TPU v7x, 32 devices: a whole 2x2x4 slice. The times are simulated.
32 devices in a mesh: dp: 8 (over z, y), fsdp: 4 (over x, core).
Axes of the slice: x: 2, y: 2, z: 4, core: 2. Of those that a mesh axis runs over, the one named last changes fastest.
Arguments:
- picture_tower_inputs: bfloat16 [16384, 1152], P(('dp', 'fsdp')), may hold values from -6 to 6
- caption_tower_inputs: bfloat16 [16384, 1152], P(('dp', 'fsdp')), may hold values from -6 to 6
- halfwidth_parameter_matrix: bfloat16 [1152, 2304], P('fsdp'), may hold values from -0.1875 to 0.1875
- affinity_multiplier: float32 [1], replicated, may hold values from 4 to 12
- affinity_offset: float32 [1], replicated, may hold values from -6 to -2
- precise_parameter_copy: float32 [1152, 2304], P('fsdp', 'dp'), may hold values from -0.125 to 0.125
- gradient_mean_estimate: float32 [1152, 2304], P('fsdp', 'dp'), may hold values from -4 to 4
- gradient_variance_estimate: float32 [1152, 2304], P('fsdp', 'dp'), may hold values from 0.05 to 1
Outputs:
- img_tangent: bfloat16 [16384, 1152], P(('dp', 'fsdp'))
- txt_tangent: bfloat16 [16384, 1152], P(('dp', 'fsdp'))
- new_master: float32 [1152, 2304], P('fsdp', 'dp')
- new_one: float32 [1152, 2304], P('fsdp', 'dp')
- new_two: float32 [1152, 2304], P('fsdp', 'dp')
- new_weights: bfloat16 [1152, 2304], P('fsdp')
All inputs are finite; a program needn't handle non-finite values.
Results may differ from a plain program's by a relative error of at most 0.008.
Values may be sent and summed in bfloat16 or wider, within the bound.
A program may use at most 128 MiB of HBM per device.

v0:
```python
import jax
import jax.numpy as jnp
from jax import lax
from jax.experimental import pallas as pl
from jax.experimental.pallas import tpu as pltpu
from jax.sharding import PartitionSpec as P

CYCLE = 4


def shifted(value, axis, steps):
    count = lax.axis_size(axis)
    pairs = [(source, (source + steps) % count) for source in range(count)]
    return lax.ppermute(value, axis, pairs)


def swapped(value, axis, bit):
    count = lax.axis_size(axis)
    return lax.ppermute(value, axis, [(source, source ^ bit) for source in range(count)])


def bit_of(axis, bit):
    return (lax.axis_index(axis) // bit) % 2 == 1


def ordered(mine, other, high):
    return jnp.where(high, other, mine), jnp.where(high, mine, other)


def project_kernel(rows_ref, weights_ref, unit_ref, low_ref, norm_ref):
    step = 128

    @pl.loop(0, rows_ref.shape[0] // step)
    def _(block):
        at = pl.ds(pl.multiple_of(block * step, step), step)
        projected = jnp.dot(
            rows_ref[at, :], weights_ref[...], preferred_element_type=jnp.float32
        )
        inv_norm = lax.rsqrt(jnp.sum(projected * projected, axis=-1, keepdims=True) + 1e-06)
        unit = projected * inv_norm
        unit_ref[at, :] = unit
        low_ref[at, :] = unit.astype(jnp.bfloat16)
        norm_ref[at, :] = inv_norm


def project(rows, weights):
    shape = (rows.shape[0], weights.shape[1])
    return pl.pallas_call(
        project_kernel,
        out_shape=(
            jax.ShapeDtypeStruct(shape, jnp.float32),
            jax.ShapeDtypeStruct(shape, jnp.bfloat16),
            jax.ShapeDtypeStruct((shape[0], 1), jnp.float32),
        ),
        in_specs=[pl.BlockSpec(memory_space=pltpu.VMEM)] * 2,
        out_specs=[pl.BlockSpec(memory_space=pltpu.VMEM)] * 3,
        compiler_params=pltpu.CompilerParams(vmem_limit_bytes=32 * 2**20),
    )(rows, weights)


def gather_kernel(own_ref, out_ref, z_send, z_recv, y_send, y_recv):
    n = out_ref.shape[0]
    steps = n // 2
    me = lax.axis_index("dp")
    after = lax.rem(me + 2, n)
    before = lax.rem(me + n - 2, n)
    beside = me + 1 - 2 * lax.rem(me, 2)
    barrier = pltpu.get_barrier_semaphore()
    for other in (after, before, beside):
        pl.semaphore_signal(
            barrier, inc=1, device_id={"dp": other}, device_id_type=pl.DeviceIdType.MESH
        )
    pl.semaphore_wait(barrier, 3)
    out_ref[me] = own_ref[...]
    along, across = [], []
    for step in range(steps):
        block = lax.rem(me - 2 * step + 2 * n, n)
        if step > 0:
            along[step - 1].wait_recv()
        for copies, target, sends, receives in (
            (along, after, z_send, z_recv),
            (across, beside, y_send, y_recv),
        ):
            if copies is along and step == steps - 1:
                continue
            copy = pltpu.make_async_remote_copy(
                src_ref=out_ref.at[block],
                dst_ref=out_ref.at[block],
                send_sem=sends.at[step],
                recv_sem=receives.at[step],
                device_id={"dp": target},
                device_id_type=pl.DeviceIdType.MESH,
            )
            copy.start()
            copies.append(copy)
    for copy in along:
        copy.wait_send()
    for copy in across:
        copy.wait()


def gather_columns(own, n_dp):
    return pl.pallas_call(
        gather_kernel,
        out_shape=jax.ShapeDtypeStruct((n_dp,) + own.shape, own.dtype),
        in_specs=[pl.BlockSpec(memory_space=pltpu.VMEM)],
        out_specs=pl.BlockSpec(memory_space=pltpu.VMEM),
        scratch_shapes=[pltpu.SemaphoreType.DMA((n_dp // 2,))] * 4,
        compiler_params=pltpu.CompilerParams(
            collective_id=0, has_side_effects=True, vmem_limit_bytes=32 * 2**20
        ),
    )(own)


def contract_rows(left, right):
    return lax.dot_general(
        left, right, (((0,), (0,)), ((), ())), preferred_element_type=jnp.float32
    )


def weigh_pairs(left, right, scale, shift, sign_label):
    logits = (
        scale
        * lax.dot_general(
            left, right, (((1,), (1,)), ((), ())), preferred_element_type=jnp.float32
        )
        + shift
    )
    return (-sign_label * jax.nn.sigmoid(-sign_label * logits) * scale).astype(jnp.bfloat16)


def gather_weights(shard):
    rows = shard.shape[0]
    half = rows // 2
    y = bit_of("dp", 1)
    x = bit_of("fsdp", 2)
    c = bit_of("fsdp", 1)
    mine = jnp.where(y, shard[half:], shard[:half])
    got = swapped(mine, "fsdp", 2)
    rest = swapped(got, "dp", 1)
    low, high = ordered(got, rest, y)
    remote = jnp.concatenate([low, high], axis=0)
    own_core = swapped(shard, "fsdp", 1)
    remote_core = swapped(remote, "fsdp", 1)
    own_pair = jnp.concatenate(ordered(shard, own_core, c), axis=0)
    remote_pair = jnp.concatenate(ordered(remote, remote_core, c), axis=0)
    return jnp.concatenate(ordered(own_pair, remote_pair, x), axis=0)


def tangent(inv_norm, unit, grad):
    return (inv_norm * (grad - unit * jnp.sum(unit * grad, axis=1, keepdims=True))).astype(
        jnp.bfloat16
    )


def gradient_kernel(img_ref, txt_ref, img_tan_ref, txt_tan_ref, order_ref, out_ref, columns_ref):
    row_count, width = img_ref.shape
    piece = out_ref.shape[-1]
    padded = columns_ref.shape[-1] // 2
    step = 384 if width % 384 == 0 else 128
    for tower, (features, rows) in enumerate(((img_ref, img_tan_ref), (txt_ref, txt_tan_ref))):
        for start in range(0, row_count, 256):
            chunk = slice(start, start + 256)
            columns_ref[chunk, :] = jnp.dot(
                rows[chunk, :], order_ref[...], preferred_element_type=jnp.float32
            ).astype(jnp.bfloat16)

        @pl.loop(0, width // step)
        def _(block):
            at = pl.multiple_of(block * step, step)
            left = features[:, pl.ds(at, step)]
            for y in range(2):
                right = columns_ref[:, y * padded : y * padded + piece]
                out_ref[y, tower, pl.ds(at, step), :] = contract_rows(left, right).astype(
                    jnp.bfloat16
                )


def weight_gradient(img, txt, img_tangent, txt_tangent, n_dp, owned):
    row_count, width = img.shape
    piece = width // 2
    padded = -(-piece // 128) * 128
    source = jnp.arange(width)
    block = source // owned
    target = (block % 2) * padded + (block // 2) * owned + source % owned
    order = (target[:, None] == jnp.arange(2 * padded)[None, :]).astype(jnp.bfloat16)
    out = pl.pallas_call(
        gradient_kernel,
        out_shape=jax.ShapeDtypeStruct((2, 2, width, piece), jnp.bfloat16),
        in_specs=[pl.BlockSpec(memory_space=pltpu.VMEM)] * 5,
        out_specs=pl.BlockSpec(memory_space=pltpu.VMEM),
        scratch_shapes=[pltpu.VMEM((row_count, 2 * padded), jnp.bfloat16)],
        compiler_params=pltpu.CompilerParams(vmem_limit_bytes=32 * 2**20),
    )(img, txt, img_tangent, txt_tangent, order)
    return [out[y, tower] for y in range(2) for tower in range(2)]


def reduce_half(value, dim, axis, bit):
    high = bit_of(axis, bit)
    low_half = lax.index_in_dim(value, 0, dim, keepdims=False)
    high_half = lax.index_in_dim(value, 1, dim, keepdims=False)
    send = jnp.where(high, low_half, high_half).astype(jnp.bfloat16)
    keep = jnp.where(high, high_half, low_half).astype(jnp.float32)
    return keep + swapped(send, axis, bit).astype(jnp.float32)


def body(
    picture_tower_inputs,
    caption_tower_inputs,
    halfwidth_parameter_matrix,
    affinity_multiplier,
    affinity_offset,
    precise_parameter_copy,
    gradient_mean_estimate,
    gradient_variance_estimate,
):
    row_count, width = picture_tower_inputs.shape
    n_dp = lax.axis_size("dp")
    scale = affinity_multiplier[0]
    shift = affinity_offset[0]

    weights_img = gather_weights(halfwidth_parameter_matrix[:, :width])
    weights_txt = gather_weights(halfwidth_parameter_matrix[:, width:])
    unit_img, low_img, norm_img = project(picture_tower_inputs, weights_img)
    unit_txt, low_txt, norm_txt = project(caption_tower_inputs, weights_txt)

    y = bit_of("dp", 1)
    cuts = 2
    size = row_count // cuts
    own_across = jnp.where(y, low_img, low_txt)
    across = [swapped(own_across[:size], "dp", 1)]
    txt_behind, img_ahead = [], []
    for i in range(cuts):
        txt_behind.append(shifted(low_txt[i * size : (i + 1) * size], "dp", 2))
        img_ahead.append(shifted(low_img[i * size : (i + 1) * size], "dp", -2))
    onward = [(s, (s + (2 if s % 2 == 0 else -2)) % n_dp) for s in range(n_dp)]
    txt_beside, img_beside, last = [], [], []
    before = across[0]
    for i in range(cuts):
        txt_behind[i], before = lax.optimization_barrier((txt_behind[i], before))
        if i == 0:
            across[0] = before
        else:
            img_beside[i - 1] = before
        beside = swapped(txt_behind[i], "dp", 1)
        if i > 0:
            last.append(lax.ppermute(jnp.where(y, img_beside[i - 1], txt_beside[i - 1]), "dp", onward))
        img_ahead[i], beside = lax.optimization_barrier((img_ahead[i], beside))
        txt_beside.append(beside)
        before = swapped(img_ahead[i], "dp", 1)
        img_beside.append(before)
    rest, img_beside[-1] = lax.optimization_barrier((own_across[size:], img_beside[-1]))
    across.append(swapped(rest, "dp", 1))
    last.append(lax.ppermute(jnp.where(y, img_beside[-1], txt_beside[-1]), "dp", onward))

    def met(own, block, sign_label=-1.0):
        pair_weight = lax.optimization_barrier(weigh_pairs(own, block, scale, shift, sign_label))
        return pair_weight, jnp.dot(pair_weight, block, preferred_element_type=jnp.float32)

    diagonal = 2.0 * jnp.eye(row_count, dtype=jnp.float32) - 1.0
    pair_weight, grad_img = met(low_img, low_txt, diagonal)
    grad_txt = contract_rows(pair_weight, low_img)
    of_across = sum(met(own_across, v)[1] for v in across)
    grad_img = grad_img + jnp.where(y, of_across, 0.0)
    grad_txt = grad_txt + jnp.where(y, 0.0, of_across)
    for t, i in zip(txt_behind + txt_beside, img_ahead + img_beside):
        grad_img = grad_img + met(low_img, t)[1]
        grad_txt = grad_txt + met(low_txt, i)[1]
    own_last = jnp.where(y, low_txt, low_img)
    of_last = sum(met(own_last, v)[1] for v in last)
    grad_img = grad_img + jnp.where(y, 0.0, of_last)
    grad_txt = grad_txt + jnp.where(y, of_last, 0.0)
    img_tangent = tangent(norm_img, unit_img, grad_img)
    txt_tangent = tangent(norm_txt, unit_txt, grad_txt)

    owned = 2 * width // n_dp
    piece = width // 2
    pieces = weight_gradient(
        picture_tower_inputs, caption_tower_inputs, img_tangent, txt_tangent, n_dp, owned
    )
    shard_rows = width // lax.axis_size("fsdp")
    half = shard_rows // 2
    split = [p.reshape(2, 2, 2, half, piece) for p in pieces]

    new_parts = []
    for part in range(2):
        total = jnp.stack([s[:, :, part] for s in split]).reshape(2, 2, 2, 2, half, piece)
        total = reduce_half(total, 3, "fsdp", 1)
        if part == 0:
            total = reduce_half(total, 2, "fsdp", 2)
            total = reduce_half(total, 0, "dp", 1)
        else:
            total = reduce_half(total, 0, "dp", 1)
            total = reduce_half(total, 1, "fsdp", 2)
        total = reduce_half(total, 0, "dp", n_dp // 2)
        bit = n_dp // 4
        while bit > 1:
            size = total.shape[-1] // 2
            total = reduce_half(jnp.stack([total[:, :size], total[:, size:]]), 0, "dp", bit)
            bit //= 2
        rows = slice(part * half, (part + 1) * half)
        new_one = 0.9 * gradient_mean_estimate[rows] + 0.1 * total
        new_two = 0.95 * gradient_variance_estimate[rows] + 0.05 * total * total
        master = precise_parameter_copy[rows]
        new_master = master - 0.001 * (new_one / (jnp.sqrt(new_two) + 1e-08) + 0.1 * master)

        new_parts.append((new_master, new_one, new_two))
    new_master, new_one, new_two = (jnp.concatenate(both, axis=0) for both in zip(*new_parts))
    gathered = gather_columns(new_master.astype(jnp.bfloat16), n_dp)
    new_weights = gathered.transpose(1, 0, 2).reshape(shard_rows, 2 * width)
    return (img_tangent, txt_tangent, new_master, new_one, new_two, new_weights)


def solution(mesh):
    return jax.shard_map(
        body,
        mesh=mesh,
        in_specs=(
            P(("dp", "fsdp"), None),
            P(("dp", "fsdp"), None),
            P("fsdp", None),
            P(),
            P(),
            P("fsdp", "dp"),
            P("fsdp", "dp"),
            P("fsdp", "dp"),
        ),
        out_specs=(
            P(("dp", "fsdp"), None),
            P(("dp", "fsdp"), None),
            P("fsdp", "dp"),
            P("fsdp", "dp"),
            P("fsdp", "dp"),
            P("fsdp", None),
        ),
        check_vma=False,
    )
```

profile of v0, /device:TPU:0, one launch (start us, length us, event | category | flops | bytes accessed | tf_op | source)
XLA Modules:
  0.0 271.9 jit_solution(8296855141656727069)
XLA Ops:
  0.7 1.5 slice_select_fusion
  2.1 3.0 %collective-permute-start.4 = (bf16[144,1152]{1,0:T(8,128)(2,1)S(1)}, bf16[144,1152]{1,0:T(8,128)(2,1)}, u32[]{:S(2)}, u32[]{:S(2)}) collective-permute-start(bf16[144,1152]{1,0:T(8,128)(2,1)S(1)} %get-tuple-element.75), channel_id=1, source_target_pairs={{0,2},{1,3},{2,0},{3,1},{4,6},{5,7},{6,4},{7,5},{8,10},{9,11},{10,... | collective-permute-start | bytes 995336 | tf_op jit(solution)/shard_map/ppermute | solution.py:19
  6.2 7.6 %collective-permute-done.4 = bf16[144,1152]{1,0:T(8,128)(2,1)} collective-permute-done((bf16[144,1152]{1,0:T(8,128)(2,1)S(1)}, bf16[144,1152]{1,0:T(8,128)(2,1)}, u32[]{:S(2)}, u32[]{:S(2)}) %collective-permute-start.4) | collective-permute-done | bytes 331808 | tf_op jit(solution)/shard_map/ppermute | solution.py:19
  13.9 2.1 collective-permute-start.5
  17.9 2.2 collective-permute-done
  20.1 1.8 collective-permute-start.1
  25.4 3.9 %collective-permute-done.1 = bf16[144,1152]{1,0:T(8,128)(2,1)S(1)} collective-permute-done((bf16[144,1152]{1,0:T(8,128)(2,1)}, bf16[144,1152]{1,0:T(8,128)(2,1)S(1)}, u32[]{:S(2)}, u32[]{:S(2)}) %collective-permute-start.1) | collective-permute-done | bytes 331808 | tf_op jit(solution)/shard_map/ppermute | solution.py:19
  32.5 2.9 %shard_map.128 = (f32[512,1152]{1,0:T(8,128)S(1)}, bf16[512,1152]{1,0:T(8,128)(2,1)S(1)}, f32[512,1]{1,0:T(8,128)S(1)}) custom-call(bf16[512,1152]{1,0:T(8,128)(2,1)S(1)} %copy-done.10, bf16[1152,1152]{1,0:T(8,128)(2,1)S(1)} %pad_maximum_fusion.3.weights_ref), custom_call_target="tpu_custom_call" | custom-call | tf_op jit(solution)/shard_map/pallas_call | solution.py:48
  39.1 2.9 %shard_map.127 = (f32[512,1152]{1,0:T(8,128)S(1)}, bf16[512,1152]{1,0:T(8,128)(2,1)S(1)}, f32[512,1]{1,0:T(8,128)S(1)}) custom-call(bf16[512,1152]{1,0:T(8,128)(2,1)S(1)} %copy-done.12, bf16[1152,1152]{1,0:T(8,128)(2,1)S(1)} %pad_maximum_fusion.2.weights_ref), custom_call_target="tpu_custom_call" | custom-call | tf_op jit(solution)/shard_map/pallas_call | solution.py:48
  44.5 1.5 collective-permute-start.8
  46.0 1.5 collective-permute-start.9
  48.7 2.2 collective-permute-start.10
  50.9 3.8 %collective-permute-start.12 = (bf16[256,1152]{1,0:T(8,128)(2,1)}, bf16[256,1152]{1,0:T(8,128)(2,1)}, u32[]{:S(2)}, u32[]{:S(2)}) collective-permute-start(bf16[256,1152]{1,0:T(8,128)(2,1)} %get-tuple-element.84), channel_id=1, source_target_pairs={{0,24},{4,28},{8,0},{12,4},{16,8},{20,12},{24,16},{28,20},{1,25},{... | collective-permute-start | bytes 1769480 | tf_op jit(solution)/shard_map/ppermute | solution.py:14
  55.8 6.8 %collective-permute-done.8 = bf16[256,1152]{1,0:T(8,128)(2,1)} collective-permute-done((bf16[256,1152]{1,0:T(8,128)(2,1)S(1)}, bf16[256,1152]{1,0:T(8,128)(2,1)}, u32[]{:S(2)}, u32[]{:S(2)}) %collective-permute-start.8) | collective-permute-done | bytes 589856 | tf_op jit(solution)/shard_map/ppermute | solution.py:14
  64.0 2.3 fusion.136
  66.6 2.1 fusion.103
  68.7 1.7 fusion.101
  70.5 29.6 %collective-permute-done.12 = bf16[256,1152]{1,0:T(8,128)(2,1)} collective-permute-done((bf16[256,1152]{1,0:T(8,128)(2,1)}, bf16[256,1152]{1,0:T(8,128)(2,1)}, u32[]{:S(2)}, u32[]{:S(2)}) %collective-permute-start.12) | collective-permute-done | bytes 589856 | tf_op jit(solution)/shard_map/ppermute | solution.py:14
  100.1 1.5 collective-permute-start.14
  101.6 1.7 fusion.95
  103.2 1.6 fusion.99
  104.9 1.6 fusion.139
  106.4 9.1 %collective-permute-done.14 = bf16[256,1152]{1,0:T(8,128)(2,1)S(1)} collective-permute-done((bf16[256,1152]{1,0:T(8,128)(2,1)}, bf16[256,1152]{1,0:T(8,128)(2,1)S(1)}, u32[]{:S(2)}, u32[]{:S(2)}) %collective-permute-start.14) | collective-permute-done | bytes 589856 | tf_op jit(solution)/shard_map/ppermute | solution.py:19
  115.5 1.5 collective-permute-start.15
  119.5 1.6 fusion.100
  121.7 1.6 fusion.138
  123.3 6.9 %collective-permute-done.15 = bf16[256,1152]{1,0:T(8,128)(2,1)S(1)} collective-permute-done((bf16[256,1152]{1,0:T(8,128)(2,1)}, bf16[256,1152]{1,0:T(8,128)(2,1)S(1)}, u32[]{:S(2)}, u32[]{:S(2)}) %collective-permute-start.15) | collective-permute-done | bytes 589856 | tf_op jit(solution)/shard_map/ppermute | solution.py:19
  130.1 1.5 collective-permute-start.16
  131.6 1.7 fusion.94
  133.9 1.6 fusion.142
  136.1 7.8 %collective-permute-done.16 = bf16[256,1152]{1,0:T(8,128)(2,1)S(1)} collective-permute-done((bf16[256,1152]{1,0:T(8,128)(2,1)}, bf16[256,1152]{1,0:T(8,128)(2,1)S(1)}, u32[]{:S(2)}, u32[]{:S(2)}) %collective-permute-start.16) | collective-permute-done | bytes 589856 | tf_op jit(solution)/shard_map/ppermute | solution.py:19
  147.8 10.5 %collective-permute-done.19 = bf16[256,1152]{1,0:T(8,128)(2,1)S(1)} collective-permute-done((bf16[256,1152]{1,0:T(8,128)(2,1)S(1)}, bf16[256,1152]{1,0:T(8,128)(2,1)S(1)}, u32[]{:S(2)}, u32[]{:S(2)}) %collective-permute-start.19) | collective-permute-done | bytes 589856 | tf_op jit(solution)/shard_map/ppermute | solution.py:254
  165.3 2.6 multiply_reduce_fusion
  167.9 2.7 %multiply_reduce_fusion.1 = (f32[512]{0:T(512)S(1)}, f32[512,1152]{1,0:T(8,128)S(1)}) fusion(f32[512,1152]{1,0:T(8,128)S(1)} %copy-done.5, f32[512,1152]{1,0:T(8,128)S(1)} %convolution_add_fusion.2, f32[512,1152]{1,0:T(8,128)S(1)} %fusion.140, f32[512,1152]{1,0:T(8,128)S(1)} %fusion.139, f32[512,1152]{1,0:T(8,128)S(1)} %fusion.138, ...), kind=kOutput, calls=%fused_computation.24 | convolution fusion | flops 307887616 | bytes 19728384 | tf_op jit(solution)/shard_map/dot_general | solution.py:258
  172.3 8.8 %shard_map.129 = bf16[2,2,1152,576]{3,2,1,0:T(8,128)(2,1)S(1)} custom-call(bf16[512,1152]{1,0:T(8,128)(2,1)S(1)} %copy-done.13, bf16[512,1152]{1,0:T(8,128)(2,1)S(1)} %copy-done.11, bf16[512,1152]{1,0:T(8,128)(2,1)S(1)} %get-tuple-element.95.img_tan_ref, bf16[512,1152]{1,0:T(8,128)(2,1)S(1)} %get-tuple-element.94.txt_tan_ref, ...), custom_call_target="tpu_custom_call" | custom-call | tf_op jit(solution)/shard_map/pallas_call | solution.py:187
  184.9 1.6 collective-permute-done.20
  188.1 1.5 collective-permute-start.21
  190.0 1.5 copy-done.14
  192.6 14.3 %collective-permute-done.21 = bf16[2,2,144,576]{3,2,1,0:T(8,128)(2,1)} collective-permute-done((bf16[2,2,144,576]{3,2,1,0:T(8,128)(2,1)}, bf16[2,2,144,576]{3,2,1,0:T(8,128)(2,1)}, u32[]{:S(2)}, u32[]{:S(2)}) %collective-permute-start.21) | collective-permute-done | bytes 663584 | tf_op jit(solution)/shard_map/ppermute | solution.py:19
  208.5 3.2 %collective-permute-done.26 = bf16[2,2,144,576]{3,2,0,1:T(8,128)(2,1)} collective-permute-done((bf16[2,2,144,576]{3,2,0,1:T(8,128)(2,1)}, bf16[2,2,144,576]{3,2,0,1:T(8,128)(2,1)}, u32[]{:S(2)}, u32[]{:S(2)}) %collective-permute-start.26) | collective-permute-done | bytes 663584 | tf_op jit(solution)/shard_map/ppermute | solution.py:19
  213.5 5.4 %collective-permute-done.22 = bf16[2,144,576]{2,1,0:T(8,128)(2,1)S(1)} collective-permute-done((bf16[2,144,576]{2,1,0:T(8,128)(2,1)S(1)}, bf16[2,144,576]{2,1,0:T(8,128)(2,1)S(1)}, u32[]{:S(2)}, u32[]{:S(2)}) %collective-permute-start.22) | collective-permute-done | bytes 331808 | tf_op jit(solution)/shard_map/ppermute | solution.py:19
  219.2 2.9 %collective-permute-done.27 = bf16[2,144,576]{2,1,0:T(8,128)(2,1)S(1)} collective-permute-done((bf16[2,144,576]{2,1,0:T(8,128)(2,1)S(1)}, bf16[2,144,576]{2,1,0:T(8,128)(2,1)S(1)}, u32[]{:S(2)}, u32[]{:S(2)}) %collective-permute-start.27) | collective-permute-done | bytes 331808 | tf_op jit(solution)/shard_map/ppermute | solution.py:19
  222.4 10.7 %collective-permute-done.23 = bf16[144,576]{1,0:T(8,128)(2,1)S(1)} collective-permute-done((bf16[144,576]{1,0:T(8,128)(2,1)S(1)}, bf16[144,576]{1,0:T(8,128)(2,1)S(1)}, u32[]{:S(2)}, u32[]{:S(2)}) %collective-permute-start.23) | collective-permute-done | bytes 165920 | tf_op jit(solution)/shard_map/ppermute | solution.py:19
  233.4 3.7 %collective-permute-done.28 = bf16[144,576]{1,0:T(8,128)(2,1)S(1)} collective-permute-done((bf16[144,576]{1,0:T(8,128)(2,1)S(1)}, bf16[144,576]{1,0:T(8,128)(2,1)S(1)}, u32[]{:S(2)}, u32[]{:S(2)}) %collective-permute-start.28) | collective-permute-done | bytes 165920 | tf_op jit(solution)/shard_map/ppermute | solution.py:19
  237.3 2.0 collective-permute-done.24
  239.4 2.8 %collective-permute-done.29 = bf16[144,288]{1,0:T(8,128)(2,1)S(1)} collective-permute-done((bf16[144,288]{1,0:T(8,128)(2,1)S(1)}, bf16[144,288]{1,0:T(8,128)(2,1)S(1)}, u32[]{:S(2)}, u32[]{:S(2)}) %collective-permute-start.29) | collective-permute-done | bytes 82976 | tf_op jit(solution)/shard_map/ppermute | solution.py:19
  243.5 24.0 %shard_map.130 = bf16[8,288,288]{2,1,0:T(8,128)(2,1)S(1)} custom-call(bf16[288,288]{1,0:T(8,128)(2,1)S(1)} %get-tuple-element.38.own_ref), custom_call_target="tpu_custom_call" | custom-call | tf_op jit(solution)/shard_map/pallas_call | solution.py:103
  268.1 2.2 reshape.114
  (159 shorter events, 49.5 us)
Async XLA Ops:
  0.6 4.5 %copy-start.17 = (bf16[288,2304]{1,0:T(8,128)(2,1)S(1)}, bf16[288,2304]{1,0:T(8,128)(2,1)}, u32[]{:S(2)}) copy-start(bf16[288,2304]{1,0:T(8,128)(2,1)} %param.10) | copy-start | bytes 3981316
  2.1 11.7 %collective-permute-start.4 = (bf16[144,1152]{1,0:T(8,128)(2,1)S(1)}, bf16[144,1152]{1,0:T(8,128)(2,1)}, u32[]{:S(2)}, u32[]{:S(2)}) collective-permute-start(bf16[144,1152]{1,0:T(8,128)(2,1)S(1)} %get-tuple-element.75), channel_id=1, source_target_pairs={{0,2},{1,3},{2,0},{3,1},{4,6},{5,7},{6,4},{7,5},{8,10},{9,11},{10,... | collective-permute-start | bytes 995336 | tf_op jit(solution)/shard_map/ppermute | solution.py:19
  6.0 17.6 %collective-permute-start.7 = (bf16[288,1152]{1,0:T(8,128)(2,1)}, bf16[288,1152]{1,0:T(8,128)(2,1)}, u32[]{:S(2)}, u32[]{:S(2)}) collective-permute-start(bf16[288,1152]{1,0:T(8,128)(2,1)} %slice.159), channel_id=1, source_target_pairs={{0,1},{1,0},{2,3},{3,2},{4,5},{5,4},{6,7},{7,6},{8,9},{9,8},{10,11... | collective-permute-start | bytes 1990664 | tf_op jit(solution)/shard_map/ppermute | solution.py:19
  6.0 14.1 %collective-permute-start = (bf16[144,1152]{1,0:T(8,128)(2,1)S(1)}, bf16[144,1152]{1,0:T(8,128)(2,1)}, u32[]{:S(2)}, u32[]{:S(2)}) collective-permute-start(bf16[144,1152]{1,0:T(8,128)(2,1)S(1)} %get-tuple-element.76), channel_id=1, source_target_pairs={{0,2},{1,3},{2,0},{3,1},{4,6},{5,7},{6,4},{7,5},{8,10},{9,11},{10,... | collective-permute-start | bytes 995336 | tf_op jit(solution)/shard_map/ppermute | solution.py:19
  13.9 8.5 %collective-permute-start.5 = (bf16[144,1152]{1,0:T(8,128)(2,1)}, bf16[144,1152]{1,0:T(8,128)(2,1)}, u32[]{:S(2)}, u32[]{:S(2)}) collective-permute-start(bf16[144,1152]{1,0:T(8,128)(2,1)} %collective-permute-done.4), channel_id=1, source_target_pairs={{0,4},{4,0},{8,12},{12,8},{16,20},{20,16},{24,28},{28,24},{1,5},{5... | collective-permute-start | bytes 995336 | tf_op jit(solution)/shard_map/ppermute | solution.py:19
  16.5 7.1 %copy-start.18 = (bf16[288,2304]{1,0:T(8,128)(2,1)S(1)}, bf16[288,2304]{1,0:T(8,128)(2,1)}, u32[]{:S(2)}) copy-start(bf16[288,2304]{1,0:T(8,128)(2,1)} %param.10) | copy-start | bytes 3981316
  20.1 9.2 %collective-permute-start.1 = (bf16[144,1152]{1,0:T(8,128)(2,1)}, bf16[144,1152]{1,0:T(8,128)(2,1)S(1)}, u32[]{:S(2)}, u32[]{:S(2)}) collective-permute-start(bf16[144,1152]{1,0:T(8,128)(2,1)} %collective-permute-done), channel_id=1, source_target_pairs={{0,4},{4,0},{8,12},{12,8},{16,20},{20,16},{24,28},{28,24},{1,5},{5... | collective-permute-start | bytes 995336 | tf_op jit(solution)/shard_map/ppermute | solution.py:19
  23.5 7.0 %collective-permute-start.6 = (bf16[288,1152]{1,0:T(8,128)(2,1)S(1)}, bf16[288,1152]{1,0:T(8,128)(2,1)S(1)}, u32[]{:S(2)}, u32[]{:S(2)}) collective-permute-start(bf16[288,1152]{1,0:T(8,128)(2,1)S(1)} %pad_maximum_fusion.9), channel_id=1, source_target_pairs={{0,1},{1,0},{2,3},{3,2},{4,5},{5,4},{6,7},{7,6},{8,9},{9,8},{10,11... | collective-permute-start | bytes 1990664 | tf_op jit(solution)/shard_map/ppermute | solution.py:19
  24.9 11.7 %collective-permute-start.3 = (bf16[288,1152]{1,0:T(8,128)(2,1)S(1)}, bf16[288,1152]{1,0:T(8,128)(2,1)S(1)}, u32[]{:S(2)}, u32[]{:S(2)}) collective-permute-start(bf16[288,1152]{1,0:T(8,128)(2,1)S(1)} %get-tuple-element.77), channel_id=1, source_target_pairs={{0,1},{1,0},{2,3},{3,2},{4,5},{5,4},{6,7},{7,6},{8,9},{9,8},{10,11... | collective-permute-start | bytes 1990664 | tf_op jit(solution)/shard_map/ppermute | solution.py:19
  30.4 6.6 %collective-permute-start.2 = (bf16[288,1152]{1,0:T(8,128)(2,1)S(1)}, bf16[288,1152]{1,0:T(8,128)(2,1)S(1)}, u32[]{:S(2)}, u32[]{:S(2)}) collective-permute-start(bf16[288,1152]{1,0:T(8,128)(2,1)S(1)} %pad_maximum_fusion.8), channel_id=1, source_target_pairs={{0,1},{1,0},{2,3},{3,2},{4,5},{5,4},{6,7},{7,6},{8,9},{9,8},{10,11... | collective-permute-start | bytes 1990664 | tf_op jit(solution)/shard_map/ppermute | solution.py:19
  35.5 28.5 %copy-start.2 = (bf16[512,1152]{1,0:T(8,128)(2,1)}, bf16[512,1152]{1,0:T(8,128)(2,1)S(1)}, u32[]{:S(2)}) copy-start(bf16[512,1152]{1,0:T(8,128)(2,1)S(1)} %get-tuple-element.24) | copy-start | bytes 3538948
  42.0 12.7 %copy-start = (bf16[512,1152]{1,0:T(8,128)(2,1)}, bf16[512,1152]{1,0:T(8,128)(2,1)S(1)}, u32[]{:S(2)}) copy-start(bf16[512,1152]{1,0:T(8,128)(2,1)S(1)} %get-tuple-element.23) | copy-start | bytes 3538948
  43.4 12.4 %copy-start.19 = (bf16[512,1152]{1,0:T(8,128)(2,1)}, bf16[512,1152]{1,0:T(8,128)(2,1)S(1)}, u32[]{:S(2)}) copy-start(bf16[512,1152]{1,0:T(8,128)(2,1)S(1)} %broadcast_select_fusion.5) | copy-start | bytes 3538948
  44.5 18.1 %collective-permute-start.8 = (bf16[256,1152]{1,0:T(8,128)(2,1)S(1)}, bf16[256,1152]{1,0:T(8,128)(2,1)}, u32[]{:S(2)}, u32[]{:S(2)}) collective-permute-start(bf16[256,1152]{1,0:T(8,128)(2,1)S(1)} %get-tuple-element.82), channel_id=1, source_target_pairs={{0,8},{4,12},{8,16},{12,20},{16,24},{20,28},{24,0},{28,4},{1,9},{5... | collective-permute-start | bytes 1769480 | tf_op jit(solution)/shard_map/ppermute | solution.py:14
  46.0 16.6 %collective-permute-start.9 = (bf16[256,1152]{1,0:T(8,128)(2,1)S(1)}, bf16[256,1152]{1,0:T(8,128)(2,1)S(1)}, u32[]{:S(2)}, u32[]{:S(2)}) collective-permute-start(bf16[256,1152]{1,0:T(8,128)(2,1)S(1)} %get-tuple-element.81), channel_id=1, source_target_pairs={{0,4},{4,0},{8,12},{12,8},{16,20},{20,16},{24,28},{28,24},{1,5},{5... | collective-permute-start | bytes 1769480 | tf_op jit(solution)/shard_map/ppermute | solution.py:19
  48.7 74.6 %collective-permute-start.10 = (bf16[256,1152]{1,0:T(8,128)(2,1)}, bf16[256,1152]{1,0:T(8,128)(2,1)}, u32[]{:S(2)}, u32[]{:S(2)}) collective-permute-start(bf16[256,1152]{1,0:T(8,128)(2,1)} %get-tuple-element.85), channel_id=1, source_target_pairs={{0,24},{4,28},{8,0},{12,4},{16,8},{20,12},{24,16},{28,20},{1,25},{... | collective-permute-start | bytes 1769480 | tf_op jit(solution)/shard_map/ppermute | solution.py:14
  50.9 55.5 %collective-permute-start.11 = (bf16[256,1152]{1,0:T(8,128)(2,1)}, bf16[256,1152]{1,0:T(8,128)(2,1)}, u32[]{:S(2)}, u32[]{:S(2)}) collective-permute-start(bf16[256,1152]{1,0:T(8,128)(2,1)} %get-tuple-element.83), channel_id=1, source_target_pairs={{0,8},{4,12},{8,16},{12,20},{16,24},{20,28},{24,0},{28,4},{1,9},{5... | collective-permute-start | bytes 1769480 | tf_op jit(solution)/shard_map/ppermute | solution.py:14
  50.9 49.1 %collective-permute-start.12 = (bf16[256,1152]{1,0:T(8,128)(2,1)}, bf16[256,1152]{1,0:T(8,128)(2,1)}, u32[]{:S(2)}, u32[]{:S(2)}) collective-permute-start(bf16[256,1152]{1,0:T(8,128)(2,1)} %get-tuple-element.84), channel_id=1, source_target_pairs={{0,24},{4,28},{8,0},{12,4},{16,8},{20,12},{24,16},{28,20},{1,25},{... | collective-permute-start | bytes 1769480 | tf_op jit(solution)/shard_map/ppermute | solution.py:14
  55.8 10.5 %copy-start.21 = (bf16[512,512]{1,0:T(8,128)(2,1)}, bf16[512,512]{1,0:T(8,128)(2,1)S(1)}, u32[]{:S(2)}) copy-start(bf16[512,512]{1,0:T(8,128)(2,1)S(1)} %fusion.19) | copy-start | bytes 1572868
  62.6 3.7 %copy-start.23 = (bf16[256,1152]{1,0:T(8,128)(2,1)}, bf16[256,1152]{1,0:T(8,128)(2,1)S(1)}, u32[]{:S(2)}) copy-start(bf16[256,1152]{1,0:T(8,128)(2,1)S(1)} %collective-permute-done.9) | copy-start | bytes 1769476
  62.6 37.5 %collective-permute-start.13 = (bf16[256,1152]{1,0:T(8,128)(2,1)}, bf16[256,1152]{1,0:T(8,128)(2,1)}, u32[]{:S(2)}, u32[]{:S(2)}) collective-permute-start(bf16[256,1152]{1,0:T(8,128)(2,1)} %collective-permute-done.8), channel_id=1, source_target_pairs={{0,4},{4,0},{8,12},{12,8},{16,20},{20,16},{24,28},{28,24},{1,5},{5... | collective-permute-start | bytes 1769480 | tf_op jit(solution)/shard_map/ppermute | solution.py:19
  66.6 2.1 copy-start.1
  68.7 32.9 %copy-start.3 = (bf16[512,1152]{1,0:T(8,128)(2,1)S(1)}, bf16[512,1152]{1,0:T(8,128)(2,1)}, u32[]{:S(2)}) copy-start(bf16[512,1152]{1,0:T(8,128)(2,1)} %copy-done.2) | copy-start | bytes 3538948
  100.1 15.5 %collective-permute-start.14 = (bf16[256,1152]{1,0:T(8,128)(2,1)}, bf16[256,1152]{1,0:T(8,128)(2,1)S(1)}, u32[]{:S(2)}, u32[]{:S(2)}) collective-permute-start(bf16[256,1152]{1,0:T(8,128)(2,1)} %collective-permute-done.12), channel_id=1, source_target_pairs={{0,4},{4,0},{8,12},{12,8},{16,20},{20,16},{24,28},{28,24},{1,5},{5... | collective-permute-start | bytes 1769480 | tf_op jit(solution)/shard_map/ppermute | solution.py:19
  115.5 14.6 %collective-permute-start.15 = (bf16[256,1152]{1,0:T(8,128)(2,1)}, bf16[256,1152]{1,0:T(8,128)(2,1)S(1)}, u32[]{:S(2)}, u32[]{:S(2)}) collective-permute-start(bf16[256,1152]{1,0:T(8,128)(2,1)} %collective-permute-done.11), channel_id=1, source_target_pairs={{0,4},{4,0},{8,12},{12,8},{16,20},{20,16},{24,28},{28,24},{1,5},{5... | collective-permute-start | bytes 1769480 | tf_op jit(solution)/shard_map/ppermute | solution.py:19
  118.2 17.3 %collective-permute-start.18 = (bf16[256,1152]{1,0:T(8,128)(2,1)S(1)}, bf16[256,1152]{1,0:T(8,128)(2,1)S(1)}, u32[]{:S(2)}, u32[]{:S(2)}) collective-permute-start(bf16[256,1152]{1,0:T(8,128)(2,1)S(1)} %broadcast_select_fusion.15), channel_id=1, source_target_pairs={{0,8},{4,28},{8,16},{12,4},{16,24},{20,12},{24,0},{28,20},{1,9},{5... | collective-permute-start | bytes 1769480 | tf_op jit(solution)/shard_map/ppermute | solution.py:247
  130.1 13.7 %collective-permute-start.16 = (bf16[256,1152]{1,0:T(8,128)(2,1)}, bf16[256,1152]{1,0:T(8,128)(2,1)S(1)}, u32[]{:S(2)}, u32[]{:S(2)}) collective-permute-start(bf16[256,1152]{1,0:T(8,128)(2,1)} %collective-permute-done.10), channel_id=1, source_target_pairs={{0,4},{4,0},{8,12},{12,8},{16,20},{20,16},{24,28},{28,24},{1,5},{5... | collective-permute-start | bytes 1769480 | tf_op jit(solution)/shard_map/ppermute | solution.py:19
  143.9 14.4 %collective-permute-start.19 = (bf16[256,1152]{1,0:T(8,128)(2,1)S(1)}, bf16[256,1152]{1,0:T(8,128)(2,1)S(1)}, u32[]{:S(2)}, u32[]{:S(2)}) collective-permute-start(bf16[256,1152]{1,0:T(8,128)(2,1)S(1)} %broadcast_select_fusion.14), channel_id=1, source_target_pairs={{0,8},{4,28},{8,16},{12,4},{16,24},{20,12},{24,0},{28,20},{1,9},{5... | collective-permute-start | bytes 1769480 | tf_op jit(solution)/shard_map/ppermute | solution.py:254
  146.1 12.8 %collective-permute-start.17 = (bf16[256,1152]{1,0:T(8,128)(2,1)S(1)}, bf16[256,1152]{1,0:T(8,128)(2,1)S(1)}, u32[]{:S(2)}, u32[]{:S(2)}) collective-permute-start(bf16[256,1152]{1,0:T(8,128)(2,1)S(1)} %copy-done.25), channel_id=1, source_target_pairs={{0,4},{4,0},{8,12},{12,8},{16,20},{20,16},{24,28},{28,24},{1,5},{5... | collective-permute-start | bytes 1769480 | tf_op jit(solution)/shard_map/ppermute | solution.py:19
  163.7 1.7 copy-start.7
  165.3 2.6 copy-start.5
  165.3 2.6 copy-start.16
  171.4 9.7 %copy-start.8 = (bf16[512,1152]{1,0:T(8,128)(2,1)}, bf16[512,1152]{1,0:T(8,128)(2,1)S(1)}, u32[]{:S(2)}) copy-start(bf16[512,1152]{1,0:T(8,128)(2,1)S(1)} %get-tuple-element.94.txt_tan_ref) | copy-start | bytes 3538948
  171.4 9.7 %copy-start.9 = (bf16[512,1152]{1,0:T(8,128)(2,1)}, bf16[512,1152]{1,0:T(8,128)(2,1)S(1)}, u32[]{:S(2)}) copy-start(bf16[512,1152]{1,0:T(8,128)(2,1)S(1)} %get-tuple-element.95.img_tan_ref) | copy-start | bytes 3538948
  183.2 3.3 %collective-permute-start.20 = (bf16[2,2,2,144,576]{4,3,1,2,0:T(8,128)(2,1)S(1)}, bf16[2,2,2,144,576]{4,3,1,2,0:T(8,128)(2,1)S(1)}, u32[]{:S(2)}, u32[]{:S(2)}) collective-permute-start(bf16[2,2,2,144,576]{4,3,1,2,0:T(8,128)(2,1)S(1)} %select_bitcast_fusion.1), channel_id=1, source_target_pairs={{0,1},{1,0},{2,3},{3,2},{4,5},{5,4},{6,7},{7,6},{8,9},{9,8},{10,11... | collective-permute-start | bytes 3981320 | tf_op jit(solution)/shard_map/ppermute | solution.py:19
  184.4 5.2 %collective-permute-start.25 = (bf16[2,2,2,144,576]{4,3,1,2,0:T(8,128)(2,1)S(1)}, bf16[2,2,2,144,576]{4,3,1,2,0:T(8,128)(2,1)S(1)}, u32[]{:S(2)}, u32[]{:S(2)}) collective-permute-start(bf16[2,2,2,144,576]{4,3,1,2,0:T(8,128)(2,1)S(1)} %select_bitcast_fusion), channel_id=1, source_target_pairs={{0,1},{1,0},{2,3},{3,2},{4,5},{5,4},{6,7},{7,6},{8,9},{9,8},{10,11... | collective-permute-start | bytes 3981320 | tf_op jit(solution)/shard_map/ppermute | solution.py:19
  188.1 18.8 %collective-permute-start.21 = (bf16[2,2,144,576]{3,2,1,0:T(8,128)(2,1)}, bf16[2,2,144,576]{3,2,1,0:T(8,128)(2,1)}, u32[]{:S(2)}, u32[]{:S(2)}) collective-permute-start(bf16[2,2,144,576]{3,2,1,0:T(8,128)(2,1)} %fusion.104), channel_id=1, source_target_pairs={{0,2},{1,3},{2,0},{3,1},{4,6},{5,7},{6,4},{7,5},{8,10},{9,11},{10,... | collective-permute-start | bytes 1990664 | tf_op jit(solution)/shard_map/ppermute | solution.py:19
  192.6 19.1 %collective-permute-start.26 = (bf16[2,2,144,576]{3,2,0,1:T(8,128)(2,1)}, bf16[2,2,144,576]{3,2,0,1:T(8,128)(2,1)}, u32[]{:S(2)}, u32[]{:S(2)}) collective-permute-start(bf16[2,2,144,576]{3,2,0,1:T(8,128)(2,1)} %fusion.105), channel_id=1, source_target_pairs={{0,4},{4,0},{8,12},{12,8},{16,20},{20,16},{24,28},{28,24},{1,5},{5... | collective-permute-start | bytes 1990664 | tf_op jit(solution)/shard_map/ppermute | solution.py:19
  206.9 4.8 %copy-start.15 = (f32[2,2,2,144,576]{4,3,1,2,0:T(8,128)S(1)}, f32[2,2,2,144,576]{4,3,1,2,0:T(8,128)}, u32[]{:S(2)}) copy-start(f32[2,2,2,144,576]{4,3,1,2,0:T(8,128)} %copy-done.14) | copy-start | bytes 7962628
  208.5 10.5 %collective-permute-start.22 = (bf16[2,144,576]{2,1,0:T(8,128)(2,1)S(1)}, bf16[2,144,576]{2,1,0:T(8,128)(2,1)S(1)}, u32[]{:S(2)}, u32[]{:S(2)}) collective-permute-start(bf16[2,144,576]{2,1,0:T(8,128)(2,1)S(1)} %fusion.106), channel_id=1, source_target_pairs={{0,4},{4,0},{8,12},{12,8},{16,20},{20,16},{24,28},{28,24},{1,5},{5... | collective-permute-start | bytes 995336 | tf_op jit(solution)/shard_map/ppermute | solution.py:19
  213.1 9.0 %collective-permute-start.27 = (bf16[2,144,576]{2,1,0:T(8,128)(2,1)S(1)}, bf16[2,144,576]{2,1,0:T(8,128)(2,1)S(1)}, u32[]{:S(2)}, u32[]{:S(2)}) collective-permute-start(bf16[2,144,576]{2,1,0:T(8,128)(2,1)S(1)} %fusion.107), channel_id=1, source_target_pairs={{0,2},{1,3},{2,0},{3,1},{4,6},{5,7},{6,4},{7,5},{8,10},{9,11},{10,... | collective-permute-start | bytes 995336 | tf_op jit(solution)/shard_map/ppermute | solution.py:19
  219.1 14.0 %collective-permute-start.23 = (bf16[144,576]{1,0:T(8,128)(2,1)S(1)}, bf16[144,576]{1,0:T(8,128)(2,1)S(1)}, u32[]{:S(2)}, u32[]{:S(2)}) collective-permute-start(bf16[144,576]{1,0:T(8,128)(2,1)S(1)} %fusion.110), channel_id=1, source_target_pairs={{0,16},{4,20},{8,24},{12,28},{16,0},{20,4},{24,8},{28,12},{1,17},{... | collective-permute-start | bytes 497672 | tf_op jit(solution)/shard_map/ppermute | solution.py:19
  222.3 19.9 %copy-start.26 = (f32[288,288]{1,0:T(8,128)S(1)}, f32[288,288]{1,0:T(8,128)}, u32[]{:S(2)}) copy-start(f32[288,288]{1,0:T(8,128)} %param.13) | copy-start | bytes 995332
  222.3 19.9 %copy-start.27 = (f32[288,288]{1,0:T(8,128)S(1)}, f32[288,288]{1,0:T(8,128)}, u32[]{:S(2)}) copy-start(f32[288,288]{1,0:T(8,128)} %param.15) | copy-start | bytes 995332
  222.3 19.9 %copy-start.28 = (f32[288,288]{1,0:T(8,128)S(1)}, f32[288,288]{1,0:T(8,128)}, u32[]{:S(2)}) copy-start(f32[288,288]{1,0:T(8,128)} %param.14) | copy-start | bytes 995332
  222.3 14.8 %collective-permute-start.28 = (bf16[144,576]{1,0:T(8,128)(2,1)S(1)}, bf16[144,576]{1,0:T(8,128)(2,1)S(1)}, u32[]{:S(2)}, u32[]{:S(2)}) collective-permute-start(bf16[144,576]{1,0:T(8,128)(2,1)S(1)} %fusion.111), channel_id=1, source_target_pairs={{0,16},{4,20},{8,24},{12,28},{16,0},{20,4},{24,8},{28,12},{1,17},{... | collective-permute-start | bytes 497672 | tf_op jit(solution)/shard_map/ppermute | solution.py:19
  233.3 6.1 %collective-permute-start.24 = (bf16[144,288]{1,0:T(8,128)(2,1)S(1)}, bf16[144,288]{1,0:T(8,128)(2,1)S(1)}, u32[]{:S(2)}, u32[]{:S(2)}) collective-permute-start(bf16[144,288]{1,0:T(8,128)(2,1)S(1)} %select_convert_fusion.7), channel_id=1, source_target_pairs={{0,8},{4,12},{8,0},{12,4},{16,24},{20,28},{24,16},{28,20},{1,9},{5... | collective-permute-start | bytes 248840 | tf_op jit(solution)/shard_map/ppermute | solution.py:19
  237.3 4.9 %collective-permute-start.29 = (bf16[144,288]{1,0:T(8,128)(2,1)S(1)}, bf16[144,288]{1,0:T(8,128)(2,1)S(1)}, u32[]{:S(2)}, u32[]{:S(2)}) collective-permute-start(bf16[144,288]{1,0:T(8,128)(2,1)S(1)} %select_convert_fusion.6), channel_id=1, source_target_pairs={{0,8},{4,12},{8,0},{12,4},{16,24},{20,28},{24,16},{28,20},{1,9},{5... | collective-permute-start | bytes 248840 | tf_op jit(solution)/shard_map/ppermute | solution.py:19
  (11 other events, 14.5 us)
where the time goes:
time: 273 us; the launch traced here: 272 us
  waiting for transfers between devices  132 us (48%)
  Pallas kernels  38.7 us (14%)
  matrix products  31.6 us (12%)
  starting transfers between devices  28.3 us (10%)
  other arithmetic  20.8 us (8%)
  local copies, waits for them, and re-layouts  18.1 us (7%)
  between operations  2.86 us (1%)
    ppermute x24, waiting for transfers between devices, swapped(): lax.ppermute(value, axis, [(source, source ^ bit) for source in range(cou...  84.7 us
    ppermute x4, waiting for transfers between devices, shifted(): return lax.ppermute(value, axis, pairs)  36.4 us
    pallas_call x1, Pallas kernels, gather_columns(): pl.pallas_call(gather_kernel, out_shape=jax.ShapeDtypeStruct((n_dp,) + ow...  24 us
    ppermute x24, starting transfers between devices, swapped(): lax.ppermute(value, axis, [(source, source ^ bit) for source in range(cou...  19.4 us
    dot_general x13, matrix products, met(): jnp.dot(pair_weight, block, preferred_element_type=jnp.float32)  15.9 us
    dot_general x13, matrix products, weigh_pairs(): lax.dot_general(left, right, (((1,), (1,)), ((), ())), preferred_element_...  14.9 us
    ppermute x1, waiting for transfers between devices, body(): lax.ppermute(jnp.where(y, img_beside[-1], txt_beside[-1]), 'dp', onward)  10.5 us
    unnamed x58, local copies, waits for them, and re-layouts  9.64 us
  transfers between devices with their start and end apart: 30, of which 19 were waited for; matrix products, arithmetic and copies ran while one was open for 15% of the time, Pallas kernels for 1%

commit v1 on v0

--- a/solution.py
+++ b/solution.py
@@ -54,7 +54,7 @@
         ),
         in_specs=[pl.BlockSpec(memory_space=pltpu.VMEM)] * 2,
         out_specs=[pl.BlockSpec(memory_space=pltpu.VMEM)] * 3,
-        compiler_params=pltpu.CompilerParams(vmem_limit_bytes=32 * 2**20),
+        compiler_params=pltpu.CompilerParams(vmem_limit_bytes=14 * 2**20),
     )(rows, weights)
 
 
@@ -107,7 +107,7 @@
         out_specs=pl.BlockSpec(memory_space=pltpu.VMEM),
         scratch_shapes=[pltpu.SemaphoreType.DMA((n_dp // 2,))] * 4,
         compiler_params=pltpu.CompilerParams(
-            collective_id=0, has_side_effects=True, vmem_limit_bytes=32 * 2**20
+            collective_id=0, has_side_effects=True, vmem_limit_bytes=6 * 2**20
         ),
     )(own)
 
@@ -190,7 +190,7 @@
         in_specs=[pl.BlockSpec(memory_space=pltpu.VMEM)] * 5,
         out_specs=pl.BlockSpec(memory_space=pltpu.VMEM),
         scratch_shapes=[pltpu.VMEM((row_count, 2 * padded), jnp.bfloat16)],
-        compiler_params=pltpu.CompilerParams(vmem_limit_bytes=32 * 2**20),
+        compiler_params=pltpu.CompilerParams(vmem_limit_bytes=22 * 2**20),
     )(img, txt, img_tangent, txt_tangent, order)
     return [out[y, tower] for y in range(2) for tower in range(2)]
 
@@ -219,10 +219,11 @@
     scale = affinity_multiplier[0]
     shift = affinity_offset[0]
 
+    weights_txt = gather_weights(halfwidth_parameter_matrix[:, width:])
     weights_img = gather_weights(halfwidth_parameter_matrix[:, :width])
-    weights_txt = gather_weights(halfwidth_parameter_matrix[:, width:])
+    unit_txt, low_txt, norm_txt = project(caption_tower_inputs, weights_txt)
+    weights_img, unit_txt = lax.optimization_barrier((weights_img, unit_txt))
     unit_img, low_img, norm_img = project(picture_tower_inputs, weights_img)
-    unit_txt, low_txt, norm_txt = project(caption_tower_inputs, weights_txt)
 
     y = bit_of("dp", 1)
     cuts = 2
@@ -231,8 +232,12 @@
     across = [swapped(own_across[:size], "dp", 1)]
     txt_behind, img_ahead = [], []
     for i in range(cuts):
-        txt_behind.append(shifted(low_txt[i * size : (i + 1) * size], "dp", 2))
-        img_ahead.append(shifted(low_img[i * size : (i + 1) * size], "dp", -2))
+        part_txt, part_img = (v[i * size : (i + 1) * size] for v in (low_txt, low_img))
+        if i > 0:
+            part_txt, txt_behind[-1] = lax.optimization_barrier((part_txt, txt_behind[-1]))
+            part_img, img_ahead[-1] = lax.optimization_barrier((part_img, img_ahead[-1]))
+        txt_behind.append(shifted(part_txt, "dp", 2))
+        img_ahead.append(shifted(part_img, "dp", -2))
     onward = [(s, (s + (2 if s % 2 == 0 else -2)) % n_dp) for s in range(n_dp)]
     txt_beside, img_beside, last = [], [], []
     before = across[0]

time: 273 us -> 268 us (0.982)
  waiting for transfers between devices: 132 us -> 109 us
  starting transfers between devices: 28.3 us -> 46.6 us
  matrix products: 31.6 us -> 27 us
  local copies, waits for them, and re-layouts: 18.1 us -> 21.5 us
    ppermute x24, waiting for transfers between devices: 84.7 us -> 70.9 us  [swapped(): lax.ppermute(value, axis, [(source, source ^ bit) for source in range(cou...]
    ppermute x24, starting transfers between devices: 19.4 us -> 29.1 us  [swapped(): lax.ppermute(value, axis, [(source, source ^ bit) for source in range(cou...]
    ppermute x4, waiting for transfers between devices: 36.4 us -> 30.8 us  [shifted(): return lax.ppermute(value, axis, pairs)]
    ppermute x1, starting transfers between devices: 0.62 us -> 6.13 us  [body(): lax.ppermute(jnp.where(y, img_beside[-1], txt_beside[-1]), 'dp', onward)]
    ppermute x1, waiting for transfers between devices: 10.5 us -> 7.02 us  [body(): lax.ppermute(jnp.where(y, img_beside[-1], txt_beside[-1]), 'dp', onward)]
  transfers between devices with their start and end apart: 30 -> 30, of which waited for: 19 -> 19; matrix products, arithmetic and copies ran while one was open for 15% -> 13% of each run, Pallas kernels for 1% -> 0%
where the time goes in v1:
time: 268 us; the launch traced here: 267 us
  waiting for transfers between devices  109 us (41%)
  starting transfers between devices  46.6 us (17%)
  Pallas kernels  39.6 us (15%)
  matrix products  27 us (10%)
  local copies, waits for them, and re-layouts  21.5 us (8%)
  other arithmetic  20.5 us (8%)
  between operations  2.7 us (1%)
    ppermute x24, waiting for transfers between devices, swapped(): lax.ppermute(value, axis, [(source, source ^ bit) for source in range(cou...  70.9 us
    ppermute x4, waiting for transfers between devices, shifted(): return lax.ppermute(value, axis, pairs)  30.8 us
    ppermute x24, starting transfers between devices, swapped(): lax.ppermute(value, axis, [(source, source ^ bit) for source in range(cou...  29.1 us
    pallas_call x1, Pallas kernels, gather_columns(): pl.pallas_call(gather_kernel, out_shape=jax.ShapeDtypeStruct((n_dp,) + ow...  24.8 us
    dot_general x13, matrix products, met(): jnp.dot(pair_weight, block, preferred_element_type=jnp.float32)  13.4 us
    dot_general x13, matrix products, weigh_pairs(): lax.dot_general(left, right, (((1,), (1,)), ((), ())), preferred_element_...  12.7 us
    ppermute x4, starting transfers between devices, shifted(): return lax.ppermute(value, axis, pairs)  9.81 us
    unnamed x58, local copies, waits for them, and re-layouts  8.96 us
  transfers between devices with their start and end apart: 30, of which 19 were waited for; matrix products, arithmetic and copies ran while one was open for 13% of the time, Pallas kernels for 0%

profile of v1, /device:TPU:0, one launch (start us, length us, event | category | flops | bytes accessed | tf_op | source)
XLA Modules:
  0.0 266.7 jit_solution(1705854360383099990)
XLA Ops:
  0.6 2.1 slice.159
  4.0 2.5 collective-permute-start
  8.4 7.0 %collective-permute-done = bf16[144,1152]{1,0:T(8,128)(2,1)} collective-permute-done((bf16[144,1152]{1,0:T(8,128)(2,1)}, bf16[144,1152]{1,0:T(8,128)(2,1)}, u32[]{:S(2)}, u32[]{:S(2)}) %collective-permute-start) | collective-permute-done | bytes 331808 | tf_op jit(solution)/shard_map/ppermute | solution.py:19
  15.4 2.0 collective-permute-start.1
  17.4 5.0 %collective-permute-done.4 = bf16[144,1152]{1,0:T(8,128)(2,1)} collective-permute-done((bf16[144,1152]{1,0:T(8,128)(2,1)S(1)}, bf16[144,1152]{1,0:T(8,128)(2,1)}, u32[]{:S(2)}, u32[]{:S(2)}) %collective-permute-start.4) | collective-permute-done | bytes 331808 | tf_op jit(solution)/shard_map/ppermute | solution.py:19
  22.4 1.8 collective-permute-start.5
  24.1 1.6 broadcast_select_fusion.7
  27.5 4.7 %collective-permute-done.5 = bf16[144,1152]{1,0:T(8,128)(2,1)S(1)} collective-permute-done((bf16[144,1152]{1,0:T(8,128)(2,1)}, bf16[144,1152]{1,0:T(8,128)(2,1)S(1)}, u32[]{:S(2)}, u32[]{:S(2)}) %collective-permute-start.5) | collective-permute-done | bytes 331808 | tf_op jit(solution)/shard_map/ppermute | solution.py:19
  37.5 2.9 %shard_map.127 = (f32[512,1152]{1,0:T(8,128)S(1)}, bf16[512,1152]{1,0:T(8,128)(2,1)S(1)}, f32[512,1]{1,0:T(8,128)S(1)}) custom-call(bf16[512,1152]{1,0:T(8,128)(2,1)S(1)} %copy-done.10, bf16[1152,1152]{1,0:T(8,128)(2,1)S(1)} %pad_maximum_fusion.3.weights_ref), custom_call_target="tpu_custom_call" | custom-call | tf_op jit(solution)/shard_map/pallas_call | solution.py:48
  42.7 3.0 %shard_map.128 = (f32[512,1152]{1,0:T(8,128)S(1)}, bf16[512,1152]{1,0:T(8,128)(2,1)S(1)}, f32[512,1]{1,0:T(8,128)S(1)}) custom-call(bf16[512,1152]{1,0:T(8,128)(2,1)S(1)} %copy-done.12, bf16[1152,1152]{1,0:T(8,128)(2,1)S(1)} %pad_maximum_fusion.2.weights_ref), custom_call_target="tpu_custom_call" | custom-call | tf_op jit(solution)/shard_map/pallas_call | solution.py:48
  48.3 1.6 collective-permute-start.8
  50.0 1.5 collective-permute-start.9
  52.6 2.3 collective-permute-start.10
  55.9 10.5 %collective-permute-done.8 = bf16[256,1152]{1,0:T(8,128)(2,1)} collective-permute-done((bf16[256,1152]{1,0:T(8,128)(2,1)S(1)}, bf16[256,1152]{1,0:T(8,128)(2,1)}, u32[]{:S(2)}, u32[]{:S(2)}) %collective-permute-start.8) | collective-permute-done | bytes 589856 | tf_op jit(solution)/shard_map/ppermute | solution.py:14
  66.4 1.6 collective-permute-start.13
  68.0 2.3 fusion.136
  70.6 7.8 %collective-permute-done.10 = bf16[256,1152]{1,0:T(8,128)(2,1)} collective-permute-done((bf16[256,1152]{1,0:T(8,128)(2,1)}, bf16[256,1152]{1,0:T(8,128)(2,1)}, u32[]{:S(2)}, u32[]{:S(2)}) %collective-permute-start.10) | collective-permute-done | bytes 589856 | tf_op jit(solution)/shard_map/ppermute | solution.py:14
  78.4 5.9 %collective-permute-start.11 = (bf16[256,1152]{1,0:T(8,128)(2,1)}, bf16[256,1152]{1,0:T(8,128)(2,1)S(1)}, u32[]{:S(2)}, u32[]{:S(2)}) collective-permute-start(bf16[256,1152]{1,0:T(8,128)(2,1)} %get-tuple-element.35), channel_id=1, source_target_pairs={{0,24},{4,28},{8,0},{12,4},{16,8},{20,12},{24,16},{28,20},{1,25},{... | collective-permute-start | bytes 1769480 | tf_op jit(solution)/shard_map/ppermute | solution.py:14
  84.3 2.1 fusion.103
  86.4 1.7 fusion.101
  88.7 1.7 fusion.95
  90.4 1.6 fusion.99
  92.0 1.6 fusion.139
  93.6 12.5 %collective-permute-done.12 = bf16[256,1152]{1,0:T(8,128)(2,1)S(1)} collective-permute-done((bf16[256,1152]{1,0:T(8,128)(2,1)}, bf16[256,1152]{1,0:T(8,128)(2,1)S(1)}, u32[]{:S(2)}, u32[]{:S(2)}) %collective-permute-start.12) | collective-permute-done | bytes 589856 | tf_op jit(solution)/shard_map/ppermute | solution.py:14
  108.7 1.6 collective-permute-start.18
  112.5 6.1 %collective-permute-done.15 = bf16[256,1152]{1,0:T(8,128)(2,1)S(1)} collective-permute-done((bf16[256,1152]{1,0:T(8,128)(2,1)S(1)}, bf16[256,1152]{1,0:T(8,128)(2,1)S(1)}, u32[]{:S(2)}, u32[]{:S(2)}) %collective-permute-start.15) | collective-permute-done | bytes 589856 | tf_op jit(solution)/shard_map/ppermute | solution.py:19
  118.6 2.5 collective-permute-start.16
  123.3 5.6 %collective-permute-done.16 = bf16[256,1152]{1,0:T(8,128)(2,1)S(1)} collective-permute-done((bf16[256,1152]{1,0:T(8,128)(2,1)S(1)}, bf16[256,1152]{1,0:T(8,128)(2,1)S(1)}, u32[]{:S(2)}, u32[]{:S(2)}) %collective-permute-start.16) | collective-permute-done | bytes 589856 | tf_op jit(solution)/shard_map/ppermute | solution.py:19
  129.0 6.1 %collective-permute-start.19 = (bf16[256,1152]{1,0:T(8,128)(2,1)S(1)}, bf16[256,1152]{1,0:T(8,128)(2,1)S(1)}, u32[]{:S(2)}, u32[]{:S(2)}) collective-permute-start(bf16[256,1152]{1,0:T(8,128)(2,1)S(1)} %broadcast_select_fusion.14), channel_id=1, source_target_pairs={{0,8},{4,28},{8,16},{12,4},{16,24},{20,12},{24,0},{28,20},{1,9},{5... | collective-permute-start | bytes 1769480 | tf_op jit(solution)/shard_map/ppermute | solution.py:259
  138.6 7.0 %collective-permute-done.19 = bf16[256,1152]{1,0:T(8,128)(2,1)S(1)} collective-permute-done((bf16[256,1152]{1,0:T(8,128)(2,1)S(1)}, bf16[256,1152]{1,0:T(8,128)(2,1)S(1)}, u32[]{:S(2)}, u32[]{:S(2)}) %collective-permute-start.19) | collective-permute-done | bytes 589856 | tf_op jit(solution)/shard_map/ppermute | solution.py:259
  146.2 2.7 collective-permute-done.17
  154.6 2.5 multiply_reduce_fusion
  157.1 2.5 multiply_reduce_fusion.1
  161.2 8.9 %shard_map.129 = bf16[2,2,1152,576]{3,2,1,0:T(8,128)(2,1)S(1)} custom-call(bf16[512,1152]{1,0:T(8,128)(2,1)S(1)} %copy-done.13, bf16[512,1152]{1,0:T(8,128)(2,1)S(1)} %copy-done.11, bf16[512,1152]{1,0:T(8,128)(2,1)S(1)} %get-tuple-element.107.img_tan_ref, bf16[512,1152]{1,0:T(8,128)(2,1)S(1)} %get-tuple-element.106.txt_tan_ref, ...), custom_call_target="tpu_custom_call" | custom-call | tf_op jit(solution)/shard_map/pallas_call | solution.py:187
  173.9 1.7 collective-permute-done.20
  179.1 1.5 copy-done.14
  182.8 13.1 %collective-permute-done.21 = bf16[2,2,144,576]{3,2,1,0:T(8,128)(2,1)} collective-permute-done((bf16[2,2,144,576]{3,2,1,0:T(8,128)(2,1)}, bf16[2,2,144,576]{3,2,1,0:T(8,128)(2,1)}, u32[]{:S(2)}, u32[]{:S(2)}) %collective-permute-start.21) | collective-permute-done | bytes 663584 | tf_op jit(solution)/shard_map/ppermute | solution.py:19
  198.6 2.2 collective-permute-done.26
  202.5 5.4 %collective-permute-done.22 = bf16[2,144,576]{2,1,0:T(8,128)(2,1)S(1)} collective-permute-done((bf16[2,144,576]{2,1,0:T(8,128)(2,1)S(1)}, bf16[2,144,576]{2,1,0:T(8,128)(2,1)S(1)}, u32[]{:S(2)}, u32[]{:S(2)}) %collective-permute-start.22) | collective-permute-done | bytes 331808 | tf_op jit(solution)/shard_map/ppermute | solution.py:19
  208.2 4.2 %collective-permute-start.23 = (bf16[144,576]{1,0:T(8,128)(2,1)S(1)}, bf16[144,576]{1,0:T(8,128)(2,1)S(1)}, u32[]{:S(2)}, u32[]{:S(2)}) collective-permute-start(bf16[144,576]{1,0:T(8,128)(2,1)S(1)} %fusion.110), channel_id=1, source_target_pairs={{0,16},{4,20},{8,24},{12,28},{16,0},{20,4},{24,8},{28,12},{1,17},{... | collective-permute-start | bytes 497672 | tf_op jit(solution)/shard_map/ppermute | solution.py:19
  212.6 3.0 %collective-permute-start.28 = (bf16[144,576]{1,0:T(8,128)(2,1)S(1)}, bf16[144,576]{1,0:T(8,128)(2,1)S(1)}, u32[]{:S(2)}, u32[]{:S(2)}) collective-permute-start(bf16[144,576]{1,0:T(8,128)(2,1)S(1)} %fusion.111), channel_id=1, source_target_pairs={{0,16},{4,20},{8,24},{12,28},{16,0},{20,4},{24,8},{28,12},{1,17},{... | collective-permute-start | bytes 497672 | tf_op jit(solution)/shard_map/ppermute | solution.py:19
  215.6 10.1 %collective-permute-done.23 = bf16[144,576]{1,0:T(8,128)(2,1)S(1)} collective-permute-done((bf16[144,576]{1,0:T(8,128)(2,1)S(1)}, bf16[144,576]{1,0:T(8,128)(2,1)S(1)}, u32[]{:S(2)}, u32[]{:S(2)}) %collective-permute-start.23) | collective-permute-done | bytes 165920 | tf_op jit(solution)/shard_map/ppermute | solution.py:19
  225.9 2.3 collective-permute-done.28
  229.1 2.4 collective-permute-done.24
  231.5 1.7 collective-permute-done.29
  234.5 24.8 %shard_map.130 = bf16[8,288,288]{2,1,0:T(8,128)(2,1)S(1)} custom-call(bf16[288,288]{1,0:T(8,128)(2,1)S(1)} %get-tuple-element.50.own_ref), custom_call_target="tpu_custom_call" | custom-call | tf_op jit(solution)/shard_map/pallas_call | solution.py:103
  259.3 1.9 copy.40
  261.2 4.0 %reshape.114 = bf16[288,2304]{1,0:T(8,128)(2,1)} reshape(bf16[288,8,288]{2,1,0:T(8,128)(2,1)} %copy.40) | data formatting | bytes 2654208 | tf_op jit(solution)/shard_map/reshape | solution.py:315
  (159 shorter events, 53.0 us)
Async XLA Ops:
  0.6 2.6 copy-start.17
  2.7 21.4 %collective-permute-start.7 = (bf16[288,1152]{1,0:T(8,128)(2,1)}, bf16[288,1152]{1,0:T(8,128)(2,1)}, u32[]{:S(2)}, u32[]{:S(2)}) collective-permute-start(bf16[288,1152]{1,0:T(8,128)(2,1)} %slice.159), channel_id=1, source_target_pairs={{0,1},{1,0},{2,3},{3,2},{4,5},{5,4},{6,7},{7,6},{8,9},{9,8},{10,11... | collective-permute-start | bytes 1990664 | tf_op jit(solution)/shard_map/ppermute | solution.py:19
  4.0 11.5 %collective-permute-start = (bf16[144,1152]{1,0:T(8,128)(2,1)}, bf16[144,1152]{1,0:T(8,128)(2,1)}, u32[]{:S(2)}, u32[]{:S(2)}) collective-permute-start(bf16[144,1152]{1,0:T(8,128)(2,1)} %get-tuple-element.88), channel_id=1, source_target_pairs={{0,2},{1,3},{2,0},{3,1},{4,6},{5,7},{6,4},{7,5},{8,10},{9,11},{10,... | collective-permute-start | bytes 995336 | tf_op jit(solution)/shard_map/ppermute | solution.py:19
  6.5 15.9 %collective-permute-start.4 = (bf16[144,1152]{1,0:T(8,128)(2,1)S(1)}, bf16[144,1152]{1,0:T(8,128)(2,1)}, u32[]{:S(2)}, u32[]{:S(2)}) collective-permute-start(bf16[144,1152]{1,0:T(8,128)(2,1)S(1)} %get-tuple-element.87), channel_id=1, source_target_pairs={{0,2},{1,3},{2,0},{3,1},{4,6},{5,7},{6,4},{7,5},{8,10},{9,11},{10,... | collective-permute-start | bytes 995336 | tf_op jit(solution)/shard_map/ppermute | solution.py:19
  15.4 10.4 %collective-permute-start.1 = (bf16[144,1152]{1,0:T(8,128)(2,1)}, bf16[144,1152]{1,0:T(8,128)(2,1)S(1)}, u32[]{:S(2)}, u32[]{:S(2)}) collective-permute-start(bf16[144,1152]{1,0:T(8,128)(2,1)} %collective-permute-done), channel_id=1, source_target_pairs={{0,4},{4,0},{8,12},{12,8},{16,20},{20,16},{24,28},{28,24},{1,5},{5... | collective-permute-start | bytes 995336 | tf_op jit(solution)/shard_map/ppermute | solution.py:19
  22.4 9.8 %collective-permute-start.5 = (bf16[144,1152]{1,0:T(8,128)(2,1)}, bf16[144,1152]{1,0:T(8,128)(2,1)S(1)}, u32[]{:S(2)}, u32[]{:S(2)}) collective-permute-start(bf16[144,1152]{1,0:T(8,128)(2,1)} %collective-permute-done.4), channel_id=1, source_target_pairs={{0,4},{4,0},{8,12},{12,8},{16,20},{20,16},{24,28},{28,24},{1,5},{5... | collective-permute-start | bytes 995336 | tf_op jit(solution)/shard_map/ppermute | solution.py:19
  25.8 7.6 %collective-permute-start.3 = (bf16[288,1152]{1,0:T(8,128)(2,1)S(1)}, bf16[288,1152]{1,0:T(8,128)(2,1)S(1)}, u32[]{:S(2)}, u32[]{:S(2)}) collective-permute-start(bf16[288,1152]{1,0:T(8,128)(2,1)S(1)} %get-tuple-element.89), channel_id=1, source_target_pairs={{0,1},{1,0},{2,3},{3,2},{4,5},{5,4},{6,7},{7,6},{8,9},{9,8},{10,11... | collective-permute-start | bytes 1990664 | tf_op jit(solution)/shard_map/ppermute | solution.py:19
  27.0 6.4 %copy-start.18 = (bf16[288,2304]{1,0:T(8,128)(2,1)S(1)}, bf16[288,2304]{1,0:T(8,128)(2,1)}, u32[]{:S(2)}) copy-start(bf16[288,2304]{1,0:T(8,128)(2,1)} %param.10) | copy-start | bytes 3981316
  27.0 6.6 %collective-permute-start.2 = (bf16[288,1152]{1,0:T(8,128)(2,1)S(1)}, bf16[288,1152]{1,0:T(8,128)(2,1)S(1)}, u32[]{:S(2)}, u32[]{:S(2)}) collective-permute-start(bf16[288,1152]{1,0:T(8,128)(2,1)S(1)} %pad_maximum_fusion.8), channel_id=1, source_target_pairs={{0,1},{1,0},{2,3},{3,2},{4,5},{5,4},{6,7},{7,6},{8,9},{9,8},{10,11... | collective-permute-start | bytes 1990664 | tf_op jit(solution)/shard_map/ppermute | solution.py:19
  33.3 2.2 collective-permute-start.6
  40.5 5.2 %copy-start.6 = (f32[512,1152]{1,0:T(8,128)}, f32[512,1152]{1,0:T(8,128)S(1)}, u32[]{:S(2)}) copy-start(f32[512,1152]{1,0:T(8,128)S(1)} %get-tuple-element.49) | copy-start | bytes 7077892
  40.5 27.6 %copy-start.2 = (bf16[512,1152]{1,0:T(8,128)(2,1)}, bf16[512,1152]{1,0:T(8,128)(2,1)S(1)}, u32[]{:S(2)}) copy-start(bf16[512,1152]{1,0:T(8,128)(2,1)S(1)} %get-tuple-element.32) | copy-start | bytes 3538948
  47.1 7.8 %copy-start = (bf16[512,1152]{1,0:T(8,128)(2,1)}, bf16[512,1152]{1,0:T(8,128)(2,1)S(1)}, u32[]{:S(2)}) copy-start(bf16[512,1152]{1,0:T(8,128)(2,1)S(1)} %get-tuple-element.31) | copy-start | bytes 3538948
  47.2 5.4 %copy-start.19 = (bf16[512,1152]{1,0:T(8,128)(2,1)}, bf16[512,1152]{1,0:T(8,128)(2,1)S(1)}, u32[]{:S(2)}) copy-start(bf16[512,1152]{1,0:T(8,128)(2,1)S(1)} %broadcast_select_fusion.5) | copy-start | bytes 3538948
  48.3 18.1 %collective-permute-start.8 = (bf16[256,1152]{1,0:T(8,128)(2,1)S(1)}, bf16[256,1152]{1,0:T(8,128)(2,1)}, u32[]{:S(2)}, u32[]{:S(2)}) collective-permute-start(bf16[256,1152]{1,0:T(8,128)(2,1)S(1)} %get-tuple-element.94), channel_id=1, source_target_pairs={{0,8},{4,12},{8,16},{12,20},{16,24},{20,28},{24,0},{28,4},{1,9},{5... | collective-permute-start | bytes 1769480 | tf_op jit(solution)/shard_map/ppermute | solution.py:14
  50.0 16.5 %collective-permute-start.9 = (bf16[256,1152]{1,0:T(8,128)(2,1)S(1)}, bf16[256,1152]{1,0:T(8,128)(2,1)S(1)}, u32[]{:S(2)}, u32[]{:S(2)}) collective-permute-start(bf16[256,1152]{1,0:T(8,128)(2,1)S(1)} %get-tuple-element.93), channel_id=1, source_target_pairs={{0,4},{4,0},{8,12},{12,8},{16,20},{20,16},{24,28},{28,24},{1,5},{5... | collective-permute-start | bytes 1769480 | tf_op jit(solution)/shard_map/ppermute | solution.py:19
  52.6 25.8 %collective-permute-start.10 = (bf16[256,1152]{1,0:T(8,128)(2,1)}, bf16[256,1152]{1,0:T(8,128)(2,1)}, u32[]{:S(2)}, u32[]{:S(2)}) collective-permute-start(bf16[256,1152]{1,0:T(8,128)(2,1)} %get-tuple-element.96), channel_id=1, source_target_pairs={{0,24},{4,28},{8,0},{12,4},{16,8},{20,12},{24,16},{28,20},{1,25},{... | collective-permute-start | bytes 1769480 | tf_op jit(solution)/shard_map/ppermute | solution.py:14
  55.9 14.4 %copy-start.21 = (bf16[512,512]{1,0:T(8,128)(2,1)}, bf16[512,512]{1,0:T(8,128)(2,1)S(1)}, u32[]{:S(2)}) copy-start(bf16[512,512]{1,0:T(8,128)(2,1)S(1)} %fusion.19) | copy-start | bytes 1572868
  66.4 3.9 %copy-start.23 = (bf16[256,1152]{1,0:T(8,128)(2,1)}, bf16[256,1152]{1,0:T(8,128)(2,1)S(1)}, u32[]{:S(2)}) copy-start(bf16[256,1152]{1,0:T(8,128)(2,1)S(1)} %collective-permute-done.9) | copy-start | bytes 1769476
  66.4 21.7 %collective-permute-start.13 = (bf16[256,1152]{1,0:T(8,128)(2,1)}, bf16[256,1152]{1,0:T(8,128)(2,1)}, u32[]{:S(2)}, u32[]{:S(2)}) collective-permute-start(bf16[256,1152]{1,0:T(8,128)(2,1)} %collective-permute-done.8), channel_id=1, source_target_pairs={{0,4},{4,0},{8,12},{12,8},{16,20},{20,16},{24,28},{28,24},{1,5},{5... | collective-permute-start | bytes 1769480 | tf_op jit(solution)/shard_map/ppermute | solution.py:19
  78.4 34.1 %collective-permute-start.11 = (bf16[256,1152]{1,0:T(8,128)(2,1)}, bf16[256,1152]{1,0:T(8,128)(2,1)S(1)}, u32[]{:S(2)}, u32[]{:S(2)}) collective-permute-start(bf16[256,1152]{1,0:T(8,128)(2,1)} %get-tuple-element.35), channel_id=1, source_target_pairs={{0,24},{4,28},{8,0},{12,4},{16,8},{20,12},{24,16},{28,20},{1,25},{... | collective-permute-start | bytes 1769480 | tf_op jit(solution)/shard_map/ppermute | solution.py:14
  84.3 21.9 %collective-permute-start.12 = (bf16[256,1152]{1,0:T(8,128)(2,1)}, bf16[256,1152]{1,0:T(8,128)(2,1)S(1)}, u32[]{:S(2)}, u32[]{:S(2)}) collective-permute-start(bf16[256,1152]{1,0:T(8,128)(2,1)} %get-tuple-element.36), channel_id=1, source_target_pairs={{0,8},{4,12},{8,16},{12,20},{16,24},{20,28},{24,0},{28,4},{1,9},{5... | collective-permute-start | bytes 1769480 | tf_op jit(solution)/shard_map/ppermute | solution.py:14
  86.4 2.3 copy-start.3
  88.1 18.0 %collective-permute-start.14 = (bf16[256,1152]{1,0:T(8,128)(2,1)}, bf16[256,1152]{1,0:T(8,128)(2,1)S(1)}, u32[]{:S(2)}, u32[]{:S(2)}) collective-permute-start(bf16[256,1152]{1,0:T(8,128)(2,1)} %collective-permute-done.10), channel_id=1, source_target_pairs={{0,4},{4,0},{8,12},{12,8},{16,20},{20,16},{24,28},{28,24},{1,5},{5... | collective-permute-start | bytes 1769480 | tf_op jit(solution)/shard_map/ppermute | solution.py:19
  106.1 12.4 %collective-permute-start.15 = (bf16[256,1152]{1,0:T(8,128)(2,1)S(1)}, bf16[256,1152]{1,0:T(8,128)(2,1)S(1)}, u32[]{:S(2)}, u32[]{:S(2)}) collective-permute-start(bf16[256,1152]{1,0:T(8,128)(2,1)S(1)} %collective-permute-done.12), channel_id=1, source_target_pairs={{0,4},{4,0},{8,12},{12,8},{16,20},{20,16},{24,28},{28,24},{1,5},{5... | collective-permute-start | bytes 1769480 | tf_op jit(solution)/shard_map/ppermute | solution.py:19
  108.7 14.0 %collective-permute-start.18 = (bf16[256,1152]{1,0:T(8,128)(2,1)S(1)}, bf16[256,1152]{1,0:T(8,128)(2,1)S(1)}, u32[]{:S(2)}, u32[]{:S(2)}) collective-permute-start(bf16[256,1152]{1,0:T(8,128)(2,1)S(1)} %broadcast_select_fusion.15), channel_id=1, source_target_pairs={{0,8},{4,28},{8,16},{12,4},{16,24},{20,12},{24,0},{28,20},{1,9},{5... | collective-permute-start | bytes 1769480 | tf_op jit(solution)/shard_map/ppermute | solution.py:252
  118.6 10.3 %collective-permute-start.16 = (bf16[256,1152]{1,0:T(8,128)(2,1)S(1)}, bf16[256,1152]{1,0:T(8,128)(2,1)S(1)}, u32[]{:S(2)}, u32[]{:S(2)}) collective-permute-start(bf16[256,1152]{1,0:T(8,128)(2,1)S(1)} %collective-permute-done.11), channel_id=1, source_target_pairs={{0,4},{4,0},{8,12},{12,8},{16,20},{20,16},{24,28},{28,24},{1,5},{5... | collective-permute-start | bytes 1769480 | tf_op jit(solution)/shard_map/ppermute | solution.py:19
  129.0 16.6 %collective-permute-start.19 = (bf16[256,1152]{1,0:T(8,128)(2,1)S(1)}, bf16[256,1152]{1,0:T(8,128)(2,1)S(1)}, u32[]{:S(2)}, u32[]{:S(2)}) collective-permute-start(bf16[256,1152]{1,0:T(8,128)(2,1)S(1)} %broadcast_select_fusion.14), channel_id=1, source_target_pairs={{0,8},{4,28},{8,16},{12,4},{16,24},{20,12},{24,0},{28,20},{1,9},{5... | collective-permute-start | bytes 1769480 | tf_op jit(solution)/shard_map/ppermute | solution.py:259
  136.7 12.2 %collective-permute-start.17 = (bf16[256,1152]{1,0:T(8,128)(2,1)S(1)}, bf16[256,1152]{1,0:T(8,128)(2,1)S(1)}, u32[]{:S(2)}, u32[]{:S(2)}) collective-permute-start(bf16[256,1152]{1,0:T(8,128)(2,1)S(1)} %copy-done.25), channel_id=1, source_target_pairs={{0,4},{4,0},{8,12},{12,8},{16,20},{20,16},{24,28},{28,24},{1,5},{5... | collective-permute-start | bytes 1769480 | tf_op jit(solution)/shard_map/ppermute | solution.py:19
  145.6 3.3 %copy-start.20 = (bf16[512,1152]{1,0:T(8,128)(2,1)S(1)}, bf16[512,1152]{1,0:T(8,128)(2,1)}, u32[]{:S(2)}) copy-start(bf16[512,1152]{1,0:T(8,128)(2,1)} %copy-done.19) | copy-start | bytes 3538948
  154.6 2.5 copy-start.5
  154.6 2.6 copy-start.16
  160.3 9.8 %copy-start.8 = (bf16[512,1152]{1,0:T(8,128)(2,1)}, bf16[512,1152]{1,0:T(8,128)(2,1)S(1)}, u32[]{:S(2)}) copy-start(bf16[512,1152]{1,0:T(8,128)(2,1)S(1)} %get-tuple-element.106.txt_tan_ref) | copy-start | bytes 3538948
  160.3 9.8 %copy-start.9 = (bf16[512,1152]{1,0:T(8,128)(2,1)}, bf16[512,1152]{1,0:T(8,128)(2,1)S(1)}, u32[]{:S(2)}) copy-start(bf16[512,1152]{1,0:T(8,128)(2,1)S(1)} %get-tuple-element.107.img_tan_ref) | copy-start | bytes 3538948
  172.3 3.3 %collective-permute-start.20 = (bf16[2,2,2,144,576]{4,3,1,2,0:T(8,128)(2,1)S(1)}, bf16[2,2,2,144,576]{4,3,1,2,0:T(8,128)(2,1)S(1)}, u32[]{:S(2)}, u32[]{:S(2)}) collective-permute-start(bf16[2,2,2,144,576]{4,3,1,2,0:T(8,128)(2,1)S(1)} %select_bitcast_fusion.1), channel_id=1, source_target_pairs={{0,1},{1,0},{2,3},{3,2},{4,5},{5,4},{6,7},{7,6},{8,9},{9,8},{10,11... | collective-permute-start | bytes 3981320 | tf_op jit(solution)/shard_map/ppermute | solution.py:19
  173.4 5.2 %collective-permute-start.25 = (bf16[2,2,2,144,576]{4,3,1,2,0:T(8,128)(2,1)S(1)}, bf16[2,2,2,144,576]{4,3,1,2,0:T(8,128)(2,1)S(1)}, u32[]{:S(2)}, u32[]{:S(2)}) collective-permute-start(bf16[2,2,2,144,576]{4,3,1,2,0:T(8,128)(2,1)S(1)} %select_bitcast_fusion), channel_id=1, source_target_pairs={{0,1},{1,0},{2,3},{3,2},{4,5},{5,4},{6,7},{7,6},{8,9},{9,8},{10,11... | collective-permute-start | bytes 3981320 | tf_op jit(solution)/shard_map/ppermute | solution.py:19
  177.1 18.8 %collective-permute-start.21 = (bf16[2,2,144,576]{3,2,1,0:T(8,128)(2,1)}, bf16[2,2,144,576]{3,2,1,0:T(8,128)(2,1)}, u32[]{:S(2)}, u32[]{:S(2)}) collective-permute-start(bf16[2,2,144,576]{3,2,1,0:T(8,128)(2,1)} %fusion.104), channel_id=1, source_target_pairs={{0,2},{1,3},{2,0},{3,1},{4,6},{5,7},{6,4},{7,5},{8,10},{9,11},{10,... | collective-permute-start | bytes 1990664 | tf_op jit(solution)/shard_map/ppermute | solution.py:19
  181.6 19.2 %collective-permute-start.26 = (bf16[2,2,144,576]{3,2,0,1:T(8,128)(2,1)}, bf16[2,2,144,576]{3,2,0,1:T(8,128)(2,1)}, u32[]{:S(2)}, u32[]{:S(2)}) collective-permute-start(bf16[2,2,144,576]{3,2,0,1:T(8,128)(2,1)} %fusion.105), channel_id=1, source_target_pairs={{0,4},{4,0},{8,12},{12,8},{16,20},{20,16},{24,28},{28,24},{1,5},{5... | collective-permute-start | bytes 1990664 | tf_op jit(solution)/shard_map/ppermute | solution.py:19
  195.9 4.9 %copy-start.15 = (f32[2,2,2,144,576]{4,3,1,2,0:T(8,128)S(1)}, f32[2,2,2,144,576]{4,3,1,2,0:T(8,128)}, u32[]{:S(2)}) copy-start(f32[2,2,2,144,576]{4,3,1,2,0:T(8,128)} %copy-done.14) | copy-start | bytes 7962628
  197.5 10.5 %collective-permute-start.22 = (bf16[2,144,576]{2,1,0:T(8,128)(2,1)S(1)}, bf16[2,144,576]{2,1,0:T(8,128)(2,1)S(1)}, u32[]{:S(2)}, u32[]{:S(2)}) collective-permute-start(bf16[2,144,576]{2,1,0:T(8,128)(2,1)S(1)} %fusion.106), channel_id=1, source_target_pairs={{0,4},{4,0},{8,12},{12,8},{16,20},{20,16},{24,28},{28,24},{1,5},{5... | collective-permute-start | bytes 995336 | tf_op jit(solution)/shard_map/ppermute | solution.py:19
  202.2 10.2 %collective-permute-start.27 = (bf16[2,144,576]{2,1,0:T(8,128)(2,1)S(1)}, bf16[2,144,576]{2,1,0:T(8,128)(2,1)S(1)}, u32[]{:S(2)}, u32[]{:S(2)}) collective-permute-start(bf16[2,144,576]{2,1,0:T(8,128)(2,1)S(1)} %fusion.107), channel_id=1, source_target_pairs={{0,2},{1,3},{2,0},{3,1},{4,6},{5,7},{6,4},{7,5},{8,10},{9,11},{10,... | collective-permute-start | bytes 995336 | tf_op jit(solution)/shard_map/ppermute | solution.py:19
  208.2 17.5 %collective-permute-start.23 = (bf16[144,576]{1,0:T(8,128)(2,1)S(1)}, bf16[144,576]{1,0:T(8,128)(2,1)S(1)}, u32[]{:S(2)}, u32[]{:S(2)}) collective-permute-start(bf16[144,576]{1,0:T(8,128)(2,1)S(1)} %fusion.110), channel_id=1, source_target_pairs={{0,16},{4,20},{8,24},{12,28},{16,0},{20,4},{24,8},{28,12},{1,17},{... | collective-permute-start | bytes 497672 | tf_op jit(solution)/shard_map/ppermute | solution.py:19
  212.6 20.6 %copy-start.26 = (f32[288,288]{1,0:T(8,128)S(1)}, f32[288,288]{1,0:T(8,128)}, u32[]{:S(2)}) copy-start(f32[288,288]{1,0:T(8,128)} %param.13) | copy-start | bytes 995332
  212.6 20.6 %copy-start.27 = (f32[288,288]{1,0:T(8,128)S(1)}, f32[288,288]{1,0:T(8,128)}, u32[]{:S(2)}) copy-start(f32[288,288]{1,0:T(8,128)} %param.15) | copy-start | bytes 995332
  212.6 20.6 %copy-start.28 = (f32[288,288]{1,0:T(8,128)S(1)}, f32[288,288]{1,0:T(8,128)}, u32[]{:S(2)}) copy-start(f32[288,288]{1,0:T(8,128)} %param.14) | copy-start | bytes 995332
  212.6 15.6 %collective-permute-start.28 = (bf16[144,576]{1,0:T(8,128)(2,1)S(1)}, bf16[144,576]{1,0:T(8,128)(2,1)S(1)}, u32[]{:S(2)}, u32[]{:S(2)}) collective-permute-start(bf16[144,576]{1,0:T(8,128)(2,1)S(1)} %fusion.111), channel_id=1, source_target_pairs={{0,16},{4,20},{8,24},{12,28},{16,0},{20,4},{24,8},{28,12},{1,17},{... | collective-permute-start | bytes 497672 | tf_op jit(solution)/shard_map/ppermute | solution.py:19
  225.9 5.6 %collective-permute-start.24 = (bf16[144,288]{1,0:T(8,128)(2,1)S(1)}, bf16[144,288]{1,0:T(8,128)(2,1)S(1)}, u32[]{:S(2)}, u32[]{:S(2)}) collective-permute-start(bf16[144,288]{1,0:T(8,128)(2,1)S(1)} %select_convert_fusion.7), channel_id=1, source_target_pairs={{0,8},{4,12},{8,0},{12,4},{16,24},{20,28},{24,16},{28,20},{1,9},{5... | collective-permute-start | bytes 248840 | tf_op jit(solution)/shard_map/ppermute | solution.py:19
  228.4 4.8 %collective-permute-start.29 = (bf16[144,288]{1,0:T(8,128)(2,1)S(1)}, bf16[144,288]{1,0:T(8,128)(2,1)S(1)}, u32[]{:S(2)}, u32[]{:S(2)}) collective-permute-start(bf16[144,288]{1,0:T(8,128)(2,1)S(1)} %select_convert_fusion.6), channel_id=1, source_target_pairs={{0,8},{4,12},{8,0},{12,4},{16,24},{20,28},{24,16},{28,20},{1,9},{5... | collective-permute-start | bytes 248840 | tf_op jit(solution)/shard_map/ppermute | solution.py:19
  (11 other events, 16.3 us)

commit v2 on v0

--- a/solution.py
+++ b/solution.py
@@ -231,8 +231,12 @@
     across = [swapped(own_across[:size], "dp", 1)]
     txt_behind, img_ahead = [], []
     for i in range(cuts):
-        txt_behind.append(shifted(low_txt[i * size : (i + 1) * size], "dp", 2))
-        img_ahead.append(shifted(low_img[i * size : (i + 1) * size], "dp", -2))
+        part_txt, part_img = (v[i * size : (i + 1) * size] for v in (low_txt, low_img))
+        if i > 0:
+            part_txt, txt_behind[-1] = lax.optimization_barrier((part_txt, txt_behind[-1]))
+            part_img, img_ahead[-1] = lax.optimization_barrier((part_img, img_ahead[-1]))
+        txt_behind.append(shifted(part_txt, "dp", 2))
+        img_ahead.append(shifted(part_img, "dp", -2))
     onward = [(s, (s + (2 if s % 2 == 0 else -2)) % n_dp) for s in range(n_dp)]
     txt_beside, img_beside, last = [], [], []
     before = across[0]

time: 273 us -> 260 us (0.952)
  waiting for transfers between devices: 132 us -> 105 us
  starting transfers between devices: 28.3 us -> 46.1 us
  matrix products: 31.6 us -> 27.4 us
    ppermute x24, waiting for transfers between devices: 84.7 us -> 67 us  [swapped(): lax.ppermute(value, axis, [(source, source ^ bit) for source in range(cou...]
    ppermute x24, starting transfers between devices: 19.4 us -> 30.6 us  [swapped(): lax.ppermute(value, axis, [(source, source ^ bit) for source in range(cou...]
    ppermute x4, waiting for transfers between devices: 36.4 us -> 31.6 us  [shifted(): return lax.ppermute(value, axis, pairs)]
    ppermute x1, waiting for transfers between devices: 10.5 us -> 6.22 us  [body(): lax.ppermute(jnp.where(y, img_beside[-1], txt_beside[-1]), 'dp', onward)]
    ppermute x1, starting transfers between devices: 0.62 us -> 4.3 us  [body(): lax.ppermute(jnp.where(y, img_beside[-1], txt_beside[-1]), 'dp', onward)]
  transfers between devices with their start and end apart: 30 -> 30, of which waited for: 19 -> 19; matrix products, arithmetic and copies ran while one was open for 15% -> 14% of each run, Pallas kernels for 1% -> 1%
where the time goes in v2:
time: 260 us; the launch traced here: 259 us
  waiting for transfers between devices  105 us (40%)
  starting transfers between devices  46.1 us (18%)
  Pallas kernels  39.3 us (15%)
  matrix products  27.4 us (11%)
  other arithmetic  20.8 us (8%)
  local copies, waits for them, and re-layouts  17.4 us (7%)
  between operations  2.84 us (1%)
    ppermute x24, waiting for transfers between devices, swapped(): lax.ppermute(value, axis, [(source, source ^ bit) for source in range(cou...  67 us
    ppermute x4, waiting for transfers between devices, shifted(): return lax.ppermute(value, axis, pairs)  31.6 us
    ppermute x24, starting transfers between devices, swapped(): lax.ppermute(value, axis, [(source, source ^ bit) for source in range(cou...  30.6 us
    pallas_call x1, Pallas kernels, gather_columns(): pl.pallas_call(gather_kernel, out_shape=jax.ShapeDtypeStruct((n_dp,) + ow...  24.6 us
    dot_general x13, matrix products, met(): jnp.dot(pair_weight, block, preferred_element_type=jnp.float32)  13.8 us
    dot_general x13, matrix products, weigh_pairs(): lax.dot_general(left, right, (((1,), (1,)), ((), ())), preferred_element_...  12.8 us
    ppermute x4, starting transfers between devices, shifted(): return lax.ppermute(value, axis, pairs)  9.64 us
    unnamed x58, local copies, waits for them, and re-layouts  8.97 us
  transfers between devices with their start and end apart: 30, of which 19 were waited for; matrix products, arithmetic and copies ran while one was open for 14% of the time, Pallas kernels for 1%

profile of v2, /device:TPU:0, one launch (start us, length us, event | category | flops | bytes accessed | tf_op | source)
XLA Modules:
  0.0 258.6 jit_solution(14043705718624181239)
XLA Ops:
  0.7 1.5 slice_select_fusion
  2.1 3.0 %collective-permute-start.4 = (bf16[144,1152]{1,0:T(8,128)(2,1)S(1)}, bf16[144,1152]{1,0:T(8,128)(2,1)}, u32[]{:S(2)}, u32[]{:S(2)}) collective-permute-start(bf16[144,1152]{1,0:T(8,128)(2,1)S(1)} %get-tuple-element.83), channel_id=1, source_target_pairs={{0,2},{1,3},{2,0},{3,1},{4,6},{5,7},{6,4},{7,5},{8,10},{9,11},{10,... | collective-permute-start | bytes 995336 | tf_op jit(solution)/shard_map/ppermute | solution.py:19
  6.2 7.6 %collective-permute-done.4 = bf16[144,1152]{1,0:T(8,128)(2,1)} collective-permute-done((bf16[144,1152]{1,0:T(8,128)(2,1)S(1)}, bf16[144,1152]{1,0:T(8,128)(2,1)}, u32[]{:S(2)}, u32[]{:S(2)}) %collective-permute-start.4) | collective-permute-done | bytes 331808 | tf_op jit(solution)/shard_map/ppermute | solution.py:19
  13.9 2.1 collective-permute-start.5
  17.9 2.2 collective-permute-done
  20.1 1.8 collective-permute-start.1
  25.4 3.9 %collective-permute-done.1 = bf16[144,1152]{1,0:T(8,128)(2,1)S(1)} collective-permute-done((bf16[144,1152]{1,0:T(8,128)(2,1)}, bf16[144,1152]{1,0:T(8,128)(2,1)S(1)}, u32[]{:S(2)}, u32[]{:S(2)}) %collective-permute-start.1) | collective-permute-done | bytes 331808 | tf_op jit(solution)/shard_map/ppermute | solution.py:19
  32.5 2.9 %shard_map.128 = (f32[512,1152]{1,0:T(8,128)S(1)}, bf16[512,1152]{1,0:T(8,128)(2,1)S(1)}, f32[512,1]{1,0:T(8,128)S(1)}) custom-call(bf16[512,1152]{1,0:T(8,128)(2,1)S(1)} %copy-done.10, bf16[1152,1152]{1,0:T(8,128)(2,1)S(1)} %pad_maximum_fusion.3.weights_ref), custom_call_target="tpu_custom_call" | custom-call | tf_op jit(solution)/shard_map/pallas_call | solution.py:48
  39.1 2.9 %shard_map.127 = (f32[512,1152]{1,0:T(8,128)S(1)}, bf16[512,1152]{1,0:T(8,128)(2,1)S(1)}, f32[512,1]{1,0:T(8,128)S(1)}) custom-call(bf16[512,1152]{1,0:T(8,128)(2,1)S(1)} %copy-done.12, bf16[1152,1152]{1,0:T(8,128)(2,1)S(1)} %pad_maximum_fusion.2.weights_ref), custom_call_target="tpu_custom_call" | custom-call | tf_op jit(solution)/shard_map/pallas_call | solution.py:48
  44.5 1.5 collective-permute-start.8
  46.0 1.5 collective-permute-start.9
  48.6 2.2 collective-permute-start.10
  51.9 10.6 %collective-permute-done.8 = bf16[256,1152]{1,0:T(8,128)(2,1)} collective-permute-done((bf16[256,1152]{1,0:T(8,128)(2,1)S(1)}, bf16[256,1152]{1,0:T(8,128)(2,1)}, u32[]{:S(2)}, u32[]{:S(2)}) %collective-permute-start.8) | collective-permute-done | bytes 589856 | tf_op jit(solution)/shard_map/ppermute | solution.py:14
  64.0 2.3 fusion.136
  66.5 8.2 %collective-permute-done.10 = bf16[256,1152]{1,0:T(8,128)(2,1)} collective-permute-done((bf16[256,1152]{1,0:T(8,128)(2,1)}, bf16[256,1152]{1,0:T(8,128)(2,1)}, u32[]{:S(2)}, u32[]{:S(2)}) %collective-permute-start.10) | collective-permute-done | bytes 589856 | tf_op jit(solution)/shard_map/ppermute | solution.py:14
  74.7 5.9 %collective-permute-start.11 = (bf16[256,1152]{1,0:T(8,128)(2,1)}, bf16[256,1152]{1,0:T(8,128)(2,1)S(1)}, u32[]{:S(2)}, u32[]{:S(2)}) collective-permute-start(bf16[256,1152]{1,0:T(8,128)(2,1)} %get-tuple-element.31), channel_id=1, source_target_pairs={{0,24},{4,28},{8,0},{12,4},{16,8},{20,12},{24,16},{28,20},{1,25},{... | collective-permute-start | bytes 1769480 | tf_op jit(solution)/shard_map/ppermute | solution.py:14
  80.6 2.1 fusion.103
  82.7 1.7 fusion.101
  85.0 1.7 fusion.95
  86.7 1.6 fusion.99
  88.4 1.6 fusion.139
  89.9 12.8 %collective-permute-done.12 = bf16[256,1152]{1,0:T(8,128)(2,1)S(1)} collective-permute-done((bf16[256,1152]{1,0:T(8,128)(2,1)}, bf16[256,1152]{1,0:T(8,128)(2,1)S(1)}, u32[]{:S(2)}, u32[]{:S(2)}) %collective-permute-start.12) | collective-permute-done | bytes 589856 | tf_op jit(solution)/shard_map/ppermute | solution.py:14
  102.7 1.6 collective-permute-start.15
  105.4 1.6 collective-permute-start.18
  109.2 6.9 %collective-permute-done.15 = bf16[256,1152]{1,0:T(8,128)(2,1)S(1)} collective-permute-done((bf16[256,1152]{1,0:T(8,128)(2,1)S(1)}, bf16[256,1152]{1,0:T(8,128)(2,1)S(1)}, u32[]{:S(2)}, u32[]{:S(2)}) %collective-permute-start.15) | collective-permute-done | bytes 589856 | tf_op jit(solution)/shard_map/ppermute | solution.py:19
  116.0 1.7 collective-permute-start.16
  120.1 5.8 %collective-permute-done.16 = bf16[256,1152]{1,0:T(8,128)(2,1)S(1)} collective-permute-done((bf16[256,1152]{1,0:T(8,128)(2,1)S(1)}, bf16[256,1152]{1,0:T(8,128)(2,1)S(1)}, u32[]{:S(2)}, u32[]{:S(2)}) %collective-permute-start.16) | collective-permute-done | bytes 589856 | tf_op jit(solution)/shard_map/ppermute | solution.py:19
  126.0 4.3 %collective-permute-start.19 = (bf16[256,1152]{1,0:T(8,128)(2,1)S(1)}, bf16[256,1152]{1,0:T(8,128)(2,1)S(1)}, u32[]{:S(2)}, u32[]{:S(2)}) collective-permute-start(bf16[256,1152]{1,0:T(8,128)(2,1)S(1)} %broadcast_select_fusion.14), channel_id=1, source_target_pairs={{0,8},{4,28},{8,16},{12,4},{16,24},{20,12},{24,0},{28,20},{1,9},{5... | collective-permute-start | bytes 1769480 | tf_op jit(solution)/shard_map/ppermute | solution.py:258
  131.9 2.0 collective-permute-start.17
  134.4 6.2 %collective-permute-done.19 = bf16[256,1152]{1,0:T(8,128)(2,1)S(1)} collective-permute-done((bf16[256,1152]{1,0:T(8,128)(2,1)S(1)}, bf16[256,1152]{1,0:T(8,128)(2,1)S(1)}, u32[]{:S(2)}, u32[]{:S(2)}) %collective-permute-start.19) | collective-permute-done | bytes 589856 | tf_op jit(solution)/shard_map/ppermute | solution.py:258
  141.2 2.4 collective-permute-done.17
  149.4 2.6 multiply_reduce_fusion
  152.0 2.7 %multiply_reduce_fusion.1 = (f32[512]{0:T(512)S(1)}, f32[512,1152]{1,0:T(8,128)S(1)}) fusion(f32[512,1152]{1,0:T(8,128)S(1)} %copy-done.5, f32[512,1152]{1,0:T(8,128)S(1)} %convolution_add_fusion.2, f32[512,1152]{1,0:T(8,128)S(1)} %fusion.140, f32[512,1152]{1,0:T(8,128)S(1)} %fusion.139, f32[512,1152]{1,0:T(8,128)S(1)} %fusion.138, ...), kind=kOutput, calls=%fused_computation.24 | convolution fusion | flops 307887616 | bytes 19728384 | tf_op jit(solution)/shard_map/dot_general | solution.py:262
  156.4 8.8 %shard_map.129 = bf16[2,2,1152,576]{3,2,1,0:T(8,128)(2,1)S(1)} custom-call(bf16[512,1152]{1,0:T(8,128)(2,1)S(1)} %copy-done.13, bf16[512,1152]{1,0:T(8,128)(2,1)S(1)} %copy-done.11, bf16[512,1152]{1,0:T(8,128)(2,1)S(1)} %get-tuple-element.103.img_tan_ref, bf16[512,1152]{1,0:T(8,128)(2,1)S(1)} %get-tuple-element.102.txt_tan_ref, ...), custom_call_target="tpu_custom_call" | custom-call | tf_op jit(solution)/shard_map/pallas_call | solution.py:187
  169.0 1.6 collective-permute-done.20
  174.1 1.5 copy-done.14
  176.7 1.8 collective-permute-start.26
  178.4 12.6 %collective-permute-done.21 = bf16[2,2,144,576]{3,2,1,0:T(8,128)(2,1)} collective-permute-done((bf16[2,2,144,576]{3,2,1,0:T(8,128)(2,1)}, bf16[2,2,144,576]{3,2,1,0:T(8,128)(2,1)}, u32[]{:S(2)}, u32[]{:S(2)}) %collective-permute-start.21) | collective-permute-done | bytes 663584 | tf_op jit(solution)/shard_map/ppermute | solution.py:19
  192.6 1.8 collective-permute-start.22
  197.6 5.4 %collective-permute-done.22 = bf16[2,144,576]{2,1,0:T(8,128)(2,1)S(1)} collective-permute-done((bf16[2,144,576]{2,1,0:T(8,128)(2,1)S(1)}, bf16[2,144,576]{2,1,0:T(8,128)(2,1)S(1)}, u32[]{:S(2)}, u32[]{:S(2)}) %collective-permute-start.22) | collective-permute-done | bytes 331808 | tf_op jit(solution)/shard_map/ppermute | solution.py:19
  203.2 4.3 %collective-permute-start.23 = (bf16[144,576]{1,0:T(8,128)(2,1)S(1)}, bf16[144,576]{1,0:T(8,128)(2,1)S(1)}, u32[]{:S(2)}, u32[]{:S(2)}) collective-permute-start(bf16[144,576]{1,0:T(8,128)(2,1)S(1)} %fusion.110), channel_id=1, source_target_pairs={{0,16},{4,20},{8,24},{12,28},{16,0},{20,4},{24,8},{28,12},{1,17},{... | collective-permute-start | bytes 497672 | tf_op jit(solution)/shard_map/ppermute | solution.py:19
  207.7 3.0 %collective-permute-start.28 = (bf16[144,576]{1,0:T(8,128)(2,1)S(1)}, bf16[144,576]{1,0:T(8,128)(2,1)S(1)}, u32[]{:S(2)}, u32[]{:S(2)}) collective-permute-start(bf16[144,576]{1,0:T(8,128)(2,1)S(1)} %fusion.111), channel_id=1, source_target_pairs={{0,16},{4,20},{8,24},{12,28},{16,0},{20,4},{24,8},{28,12},{1,17},{... | collective-permute-start | bytes 497672 | tf_op jit(solution)/shard_map/ppermute | solution.py:19
  210.7 10.1 %collective-permute-done.23 = bf16[144,576]{1,0:T(8,128)(2,1)S(1)} collective-permute-done((bf16[144,576]{1,0:T(8,128)(2,1)S(1)}, bf16[144,576]{1,0:T(8,128)(2,1)S(1)}, u32[]{:S(2)}, u32[]{:S(2)}) %collective-permute-start.23) | collective-permute-done | bytes 165920 | tf_op jit(solution)/shard_map/ppermute | solution.py:19
  221.0 2.3 collective-permute-done.28
  224.1 2.6 collective-permute-done.24
  226.7 1.6 collective-permute-done.29
  229.5 24.6 %shard_map.130 = bf16[8,288,288]{2,1,0:T(8,128)(2,1)S(1)} custom-call(bf16[288,288]{1,0:T(8,128)(2,1)S(1)} %get-tuple-element.46.own_ref), custom_call_target="tpu_custom_call" | custom-call | tf_op jit(solution)/shard_map/pallas_call | solution.py:103
  254.8 2.2 reshape.114
  (159 shorter events, 52.0 us)
Async XLA Ops:
  0.6 4.5 %copy-start.17 = (bf16[288,2304]{1,0:T(8,128)(2,1)S(1)}, bf16[288,2304]{1,0:T(8,128)(2,1)}, u32[]{:S(2)}) copy-start(bf16[288,2304]{1,0:T(8,128)(2,1)} %param.10) | copy-start | bytes 3981316
  2.1 11.7 %collective-permute-start.4 = (bf16[144,1152]{1,0:T(8,128)(2,1)S(1)}, bf16[144,1152]{1,0:T(8,128)(2,1)}, u32[]{:S(2)}, u32[]{:S(2)}) collective-permute-start(bf16[144,1152]{1,0:T(8,128)(2,1)S(1)} %get-tuple-element.83), channel_id=1, source_target_pairs={{0,2},{1,3},{2,0},{3,1},{4,6},{5,7},{6,4},{7,5},{8,10},{9,11},{10,... | collective-permute-start | bytes 995336 | tf_op jit(solution)/shard_map/ppermute | solution.py:19
  6.0 17.6 %collective-permute-start.7 = (bf16[288,1152]{1,0:T(8,128)(2,1)}, bf16[288,1152]{1,0:T(8,128)(2,1)}, u32[]{:S(2)}, u32[]{:S(2)}) collective-permute-start(bf16[288,1152]{1,0:T(8,128)(2,1)} %slice.159), channel_id=1, source_target_pairs={{0,1},{1,0},{2,3},{3,2},{4,5},{5,4},{6,7},{7,6},{8,9},{9,8},{10,11... | collective-permute-start | bytes 1990664 | tf_op jit(solution)/shard_map/ppermute | solution.py:19
  6.0 14.1 %collective-permute-start = (bf16[144,1152]{1,0:T(8,128)(2,1)S(1)}, bf16[144,1152]{1,0:T(8,128)(2,1)}, u32[]{:S(2)}, u32[]{:S(2)}) collective-permute-start(bf16[144,1152]{1,0:T(8,128)(2,1)S(1)} %get-tuple-element.84), channel_id=1, source_target_pairs={{0,2},{1,3},{2,0},{3,1},{4,6},{5,7},{6,4},{7,5},{8,10},{9,11},{10,... | collective-permute-start | bytes 995336 | tf_op jit(solution)/shard_map/ppermute | solution.py:19
  13.9 8.5 %collective-permute-start.5 = (bf16[144,1152]{1,0:T(8,128)(2,1)}, bf16[144,1152]{1,0:T(8,128)(2,1)}, u32[]{:S(2)}, u32[]{:S(2)}) collective-permute-start(bf16[144,1152]{1,0:T(8,128)(2,1)} %collective-permute-done.4), channel_id=1, source_target_pairs={{0,4},{4,0},{8,12},{12,8},{16,20},{20,16},{24,28},{28,24},{1,5},{5... | collective-permute-start | bytes 995336 | tf_op jit(solution)/shard_map/ppermute | solution.py:19
  16.5 7.1 %copy-start.18 = (bf16[288,2304]{1,0:T(8,128)(2,1)S(1)}, bf16[288,2304]{1,0:T(8,128)(2,1)}, u32[]{:S(2)}) copy-start(bf16[288,2304]{1,0:T(8,128)(2,1)} %param.10) | copy-start | bytes 3981316
  20.1 9.2 %collective-permute-start.1 = (bf16[144,1152]{1,0:T(8,128)(2,1)}, bf16[144,1152]{1,0:T(8,128)(2,1)S(1)}, u32[]{:S(2)}, u32[]{:S(2)}) collective-permute-start(bf16[144,1152]{1,0:T(8,128)(2,1)} %collective-permute-done), channel_id=1, source_target_pairs={{0,4},{4,0},{8,12},{12,8},{16,20},{20,16},{24,28},{28,24},{1,5},{5... | collective-permute-start | bytes 995336 | tf_op jit(solution)/shard_map/ppermute | solution.py:19
  23.5 7.0 %collective-permute-start.6 = (bf16[288,1152]{1,0:T(8,128)(2,1)S(1)}, bf16[288,1152]{1,0:T(8,128)(2,1)S(1)}, u32[]{:S(2)}, u32[]{:S(2)}) collective-permute-start(bf16[288,1152]{1,0:T(8,128)(2,1)S(1)} %pad_maximum_fusion.9), channel_id=1, source_target_pairs={{0,1},{1,0},{2,3},{3,2},{4,5},{5,4},{6,7},{7,6},{8,9},{9,8},{10,11... | collective-permute-start | bytes 1990664 | tf_op jit(solution)/shard_map/ppermute | solution.py:19
  24.9 11.7 %collective-permute-start.3 = (bf16[288,1152]{1,0:T(8,128)(2,1)S(1)}, bf16[288,1152]{1,0:T(8,128)(2,1)S(1)}, u32[]{:S(2)}, u32[]{:S(2)}) collective-permute-start(bf16[288,1152]{1,0:T(8,128)(2,1)S(1)} %get-tuple-element.85), channel_id=1, source_target_pairs={{0,1},{1,0},{2,3},{3,2},{4,5},{5,4},{6,7},{7,6},{8,9},{9,8},{10,11... | collective-permute-start | bytes 1990664 | tf_op jit(solution)/shard_map/ppermute | solution.py:19
  30.4 6.6 %collective-permute-start.2 = (bf16[288,1152]{1,0:T(8,128)(2,1)S(1)}, bf16[288,1152]{1,0:T(8,128)(2,1)S(1)}, u32[]{:S(2)}, u32[]{:S(2)}) collective-permute-start(bf16[288,1152]{1,0:T(8,128)(2,1)S(1)} %pad_maximum_fusion.8), channel_id=1, source_target_pairs={{0,1},{1,0},{2,3},{3,2},{4,5},{5,4},{6,7},{7,6},{8,9},{9,8},{10,11... | collective-permute-start | bytes 1990664 | tf_op jit(solution)/shard_map/ppermute | solution.py:19
  35.5 28.5 %copy-start.2 = (bf16[512,1152]{1,0:T(8,128)(2,1)}, bf16[512,1152]{1,0:T(8,128)(2,1)S(1)}, u32[]{:S(2)}) copy-start(bf16[512,1152]{1,0:T(8,128)(2,1)S(1)} %get-tuple-element.28) | copy-start | bytes 3538948
  42.0 8.8 %copy-start = (bf16[512,1152]{1,0:T(8,128)(2,1)}, bf16[512,1152]{1,0:T(8,128)(2,1)S(1)}, u32[]{:S(2)}) copy-start(bf16[512,1152]{1,0:T(8,128)(2,1)S(1)} %get-tuple-element.27) | copy-start | bytes 3538948
  43.4 8.5 %copy-start.19 = (bf16[512,1152]{1,0:T(8,128)(2,1)}, bf16[512,1152]{1,0:T(8,128)(2,1)S(1)}, u32[]{:S(2)}) copy-start(bf16[512,1152]{1,0:T(8,128)(2,1)S(1)} %broadcast_select_fusion.5) | copy-start | bytes 3538948
  44.5 18.1 %collective-permute-start.8 = (bf16[256,1152]{1,0:T(8,128)(2,1)S(1)}, bf16[256,1152]{1,0:T(8,128)(2,1)}, u32[]{:S(2)}, u32[]{:S(2)}) collective-permute-start(bf16[256,1152]{1,0:T(8,128)(2,1)S(1)} %get-tuple-element.90), channel_id=1, source_target_pairs={{0,8},{4,12},{8,16},{12,20},{16,24},{20,28},{24,0},{28,4},{1,9},{5... | collective-permute-start | bytes 1769480 | tf_op jit(solution)/shard_map/ppermute | solution.py:14
  46.0 16.6 %collective-permute-start.9 = (bf16[256,1152]{1,0:T(8,128)(2,1)S(1)}, bf16[256,1152]{1,0:T(8,128)(2,1)S(1)}, u32[]{:S(2)}, u32[]{:S(2)}) collective-permute-start(bf16[256,1152]{1,0:T(8,128)(2,1)S(1)} %get-tuple-element.89), channel_id=1, source_target_pairs={{0,4},{4,0},{8,12},{12,8},{16,20},{20,16},{24,28},{28,24},{1,5},{5... | collective-permute-start | bytes 1769480 | tf_op jit(solution)/shard_map/ppermute | solution.py:19
  48.6 26.1 %collective-permute-start.10 = (bf16[256,1152]{1,0:T(8,128)(2,1)}, bf16[256,1152]{1,0:T(8,128)(2,1)}, u32[]{:S(2)}, u32[]{:S(2)}) collective-permute-start(bf16[256,1152]{1,0:T(8,128)(2,1)} %get-tuple-element.92), channel_id=1, source_target_pairs={{0,24},{4,28},{8,0},{12,4},{16,8},{20,12},{24,16},{28,20},{1,25},{... | collective-permute-start | bytes 1769480 | tf_op jit(solution)/shard_map/ppermute | solution.py:14
  51.9 14.3 %copy-start.21 = (bf16[512,512]{1,0:T(8,128)(2,1)}, bf16[512,512]{1,0:T(8,128)(2,1)S(1)}, u32[]{:S(2)}) copy-start(bf16[512,512]{1,0:T(8,128)(2,1)S(1)} %fusion.19) | copy-start | bytes 1572868
  62.5 3.7 %copy-start.23 = (bf16[256,1152]{1,0:T(8,128)(2,1)}, bf16[256,1152]{1,0:T(8,128)(2,1)S(1)}, u32[]{:S(2)}) copy-start(bf16[256,1152]{1,0:T(8,128)(2,1)S(1)} %collective-permute-done.9) | copy-start | bytes 1769476
  62.5 21.9 %collective-permute-start.13 = (bf16[256,1152]{1,0:T(8,128)(2,1)}, bf16[256,1152]{1,0:T(8,128)(2,1)}, u32[]{:S(2)}, u32[]{:S(2)}) collective-permute-start(bf16[256,1152]{1,0:T(8,128)(2,1)} %collective-permute-done.8), channel_id=1, source_target_pairs={{0,4},{4,0},{8,12},{12,8},{16,20},{20,16},{24,28},{28,24},{1,5},{5... | collective-permute-start | bytes 1769480 | tf_op jit(solution)/shard_map/ppermute | solution.py:19
  74.7 34.5 %collective-permute-start.11 = (bf16[256,1152]{1,0:T(8,128)(2,1)}, bf16[256,1152]{1,0:T(8,128)(2,1)S(1)}, u32[]{:S(2)}, u32[]{:S(2)}) collective-permute-start(bf16[256,1152]{1,0:T(8,128)(2,1)} %get-tuple-element.31), channel_id=1, source_target_pairs={{0,24},{4,28},{8,0},{12,4},{16,8},{20,12},{24,16},{28,20},{1,25},{... | collective-permute-start | bytes 1769480 | tf_op jit(solution)/shard_map/ppermute | solution.py:14
  80.6 22.1 %collective-permute-start.12 = (bf16[256,1152]{1,0:T(8,128)(2,1)}, bf16[256,1152]{1,0:T(8,128)(2,1)S(1)}, u32[]{:S(2)}, u32[]{:S(2)}) collective-permute-start(bf16[256,1152]{1,0:T(8,128)(2,1)} %get-tuple-element.32), channel_id=1, source_target_pairs={{0,8},{4,12},{8,16},{12,20},{16,24},{20,28},{24,0},{28,4},{1,9},{5... | collective-permute-start | bytes 1769480 | tf_op jit(solution)/shard_map/ppermute | solution.py:14
  80.6 2.1 copy-start.1
  82.7 2.3 copy-start.3
  84.5 18.3 %collective-permute-start.14 = (bf16[256,1152]{1,0:T(8,128)(2,1)}, bf16[256,1152]{1,0:T(8,128)(2,1)S(1)}, u32[]{:S(2)}, u32[]{:S(2)}) collective-permute-start(bf16[256,1152]{1,0:T(8,128)(2,1)} %collective-permute-done.10), channel_id=1, source_target_pairs={{0,4},{4,0},{8,12},{12,8},{16,20},{20,16},{24,28},{28,24},{1,5},{5... | collective-permute-start | bytes 1769480 | tf_op jit(solution)/shard_map/ppermute | solution.py:19
  102.7 13.3 %collective-permute-start.15 = (bf16[256,1152]{1,0:T(8,128)(2,1)S(1)}, bf16[256,1152]{1,0:T(8,128)(2,1)S(1)}, u32[]{:S(2)}, u32[]{:S(2)}) collective-permute-start(bf16[256,1152]{1,0:T(8,128)(2,1)S(1)} %collective-permute-done.12), channel_id=1, source_target_pairs={{0,4},{4,0},{8,12},{12,8},{16,20},{20,16},{24,28},{28,24},{1,5},{5... | collective-permute-start | bytes 1769480 | tf_op jit(solution)/shard_map/ppermute | solution.py:19
  105.4 14.0 %collective-permute-start.18 = (bf16[256,1152]{1,0:T(8,128)(2,1)S(1)}, bf16[256,1152]{1,0:T(8,128)(2,1)S(1)}, u32[]{:S(2)}, u32[]{:S(2)}) collective-permute-start(bf16[256,1152]{1,0:T(8,128)(2,1)S(1)} %broadcast_select_fusion.15), channel_id=1, source_target_pairs={{0,8},{4,28},{8,16},{12,4},{16,24},{20,12},{24,0},{28,20},{1,9},{5... | collective-permute-start | bytes 1769480 | tf_op jit(solution)/shard_map/ppermute | solution.py:251
  116.0 9.9 %collective-permute-start.16 = (bf16[256,1152]{1,0:T(8,128)(2,1)S(1)}, bf16[256,1152]{1,0:T(8,128)(2,1)S(1)}, u32[]{:S(2)}, u32[]{:S(2)}) collective-permute-start(bf16[256,1152]{1,0:T(8,128)(2,1)S(1)} %collective-permute-done.11), channel_id=1, source_target_pairs={{0,4},{4,0},{8,12},{12,8},{16,20},{20,16},{24,28},{28,24},{1,5},{5... | collective-permute-start | bytes 1769480 | tf_op jit(solution)/shard_map/ppermute | solution.py:19
  126.0 14.6 %collective-permute-start.19 = (bf16[256,1152]{1,0:T(8,128)(2,1)S(1)}, bf16[256,1152]{1,0:T(8,128)(2,1)S(1)}, u32[]{:S(2)}, u32[]{:S(2)}) collective-permute-start(bf16[256,1152]{1,0:T(8,128)(2,1)S(1)} %broadcast_select_fusion.14), channel_id=1, source_target_pairs={{0,8},{4,28},{8,16},{12,4},{16,24},{20,12},{24,0},{28,20},{1,9},{5... | collective-permute-start | bytes 1769480 | tf_op jit(solution)/shard_map/ppermute | solution.py:258
  131.9 11.8 %collective-permute-start.17 = (bf16[256,1152]{1,0:T(8,128)(2,1)S(1)}, bf16[256,1152]{1,0:T(8,128)(2,1)S(1)}, u32[]{:S(2)}, u32[]{:S(2)}) collective-permute-start(bf16[256,1152]{1,0:T(8,128)(2,1)S(1)} %copy-done.25), channel_id=1, source_target_pairs={{0,4},{4,0},{8,12},{12,8},{16,20},{20,16},{24,28},{28,24},{1,5},{5... | collective-permute-start | bytes 1769480 | tf_op jit(solution)/shard_map/ppermute | solution.py:19
  140.7 3.0 %copy-start.20 = (bf16[512,1152]{1,0:T(8,128)(2,1)S(1)}, bf16[512,1152]{1,0:T(8,128)(2,1)}, u32[]{:S(2)}) copy-start(bf16[512,1152]{1,0:T(8,128)(2,1)} %copy-done.19) | copy-start | bytes 3538948
  149.4 2.6 %copy-start.5 = (f32[512,1152]{1,0:T(8,128)S(1)}, f32[512,1152]{1,0:T(8,128)}, u32[]{:S(2)}) copy-start(f32[512,1152]{1,0:T(8,128)} %copy-done.4) | copy-start | bytes 7077892
  149.4 2.6 %copy-start.16 = (f32[512,1152]{1,0:T(8,128)S(1)}, f32[512,1152]{1,0:T(8,128)}, u32[]{:S(2)}) copy-start(f32[512,1152]{1,0:T(8,128)} %fusion.136) | copy-start | bytes 7077892
  155.5 9.7 %copy-start.8 = (bf16[512,1152]{1,0:T(8,128)(2,1)}, bf16[512,1152]{1,0:T(8,128)(2,1)S(1)}, u32[]{:S(2)}) copy-start(bf16[512,1152]{1,0:T(8,128)(2,1)S(1)} %get-tuple-element.102.txt_tan_ref) | copy-start | bytes 3538948
  155.5 9.7 %copy-start.9 = (bf16[512,1152]{1,0:T(8,128)(2,1)}, bf16[512,1152]{1,0:T(8,128)(2,1)S(1)}, u32[]{:S(2)}) copy-start(bf16[512,1152]{1,0:T(8,128)(2,1)S(1)} %get-tuple-element.103.img_tan_ref) | copy-start | bytes 3538948
  167.4 3.3 %collective-permute-start.20 = (bf16[2,2,2,144,576]{4,3,1,2,0:T(8,128)(2,1)S(1)}, bf16[2,2,2,144,576]{4,3,1,2,0:T(8,128)(2,1)S(1)}, u32[]{:S(2)}, u32[]{:S(2)}) collective-permute-start(bf16[2,2,2,144,576]{4,3,1,2,0:T(8,128)(2,1)S(1)} %select_bitcast_fusion.1), channel_id=1, source_target_pairs={{0,1},{1,0},{2,3},{3,2},{4,5},{5,4},{6,7},{7,6},{8,9},{9,8},{10,11... | collective-permute-start | bytes 3981320 | tf_op jit(solution)/shard_map/ppermute | solution.py:19
  168.5 5.1 %collective-permute-start.25 = (bf16[2,2,2,144,576]{4,3,1,2,0:T(8,128)(2,1)S(1)}, bf16[2,2,2,144,576]{4,3,1,2,0:T(8,128)(2,1)S(1)}, u32[]{:S(2)}, u32[]{:S(2)}) collective-permute-start(bf16[2,2,2,144,576]{4,3,1,2,0:T(8,128)(2,1)S(1)} %select_bitcast_fusion), channel_id=1, source_target_pairs={{0,1},{1,0},{2,3},{3,2},{4,5},{5,4},{6,7},{7,6},{8,9},{9,8},{10,11... | collective-permute-start | bytes 3981320 | tf_op jit(solution)/shard_map/ppermute | solution.py:19
  172.2 18.8 %collective-permute-start.21 = (bf16[2,2,144,576]{3,2,1,0:T(8,128)(2,1)}, bf16[2,2,144,576]{3,2,1,0:T(8,128)(2,1)}, u32[]{:S(2)}, u32[]{:S(2)}) collective-permute-start(bf16[2,2,144,576]{3,2,1,0:T(8,128)(2,1)} %fusion.104), channel_id=1, source_target_pairs={{0,2},{1,3},{2,0},{3,1},{4,6},{5,7},{6,4},{7,5},{8,10},{9,11},{10,... | collective-permute-start | bytes 1990664 | tf_op jit(solution)/shard_map/ppermute | solution.py:19
  176.7 19.1 %collective-permute-start.26 = (bf16[2,2,144,576]{3,2,0,1:T(8,128)(2,1)}, bf16[2,2,144,576]{3,2,0,1:T(8,128)(2,1)}, u32[]{:S(2)}, u32[]{:S(2)}) collective-permute-start(bf16[2,2,144,576]{3,2,0,1:T(8,128)(2,1)} %fusion.105), channel_id=1, source_target_pairs={{0,4},{4,0},{8,12},{12,8},{16,20},{20,16},{24,28},{28,24},{1,5},{5... | collective-permute-start | bytes 1990664 | tf_op jit(solution)/shard_map/ppermute | solution.py:19
  191.0 4.8 %copy-start.15 = (f32[2,2,2,144,576]{4,3,1,2,0:T(8,128)S(1)}, f32[2,2,2,144,576]{4,3,1,2,0:T(8,128)}, u32[]{:S(2)}) copy-start(f32[2,2,2,144,576]{4,3,1,2,0:T(8,128)} %copy-done.14) | copy-start | bytes 7962628
  192.6 10.5 %collective-permute-start.22 = (bf16[2,144,576]{2,1,0:T(8,128)(2,1)S(1)}, bf16[2,144,576]{2,1,0:T(8,128)(2,1)S(1)}, u32[]{:S(2)}, u32[]{:S(2)}) collective-permute-start(bf16[2,144,576]{2,1,0:T(8,128)(2,1)S(1)} %fusion.106), channel_id=1, source_target_pairs={{0,4},{4,0},{8,12},{12,8},{16,20},{20,16},{24,28},{28,24},{1,5},{5... | collective-permute-start | bytes 995336 | tf_op jit(solution)/shard_map/ppermute | solution.py:19
  197.2 10.3 %collective-permute-start.27 = (bf16[2,144,576]{2,1,0:T(8,128)(2,1)S(1)}, bf16[2,144,576]{2,1,0:T(8,128)(2,1)S(1)}, u32[]{:S(2)}, u32[]{:S(2)}) collective-permute-start(bf16[2,144,576]{2,1,0:T(8,128)(2,1)S(1)} %fusion.107), channel_id=1, source_target_pairs={{0,2},{1,3},{2,0},{3,1},{4,6},{5,7},{6,4},{7,5},{8,10},{9,11},{10,... | collective-permute-start | bytes 995336 | tf_op jit(solution)/shard_map/ppermute | solution.py:19
  203.2 17.6 %collective-permute-start.23 = (bf16[144,576]{1,0:T(8,128)(2,1)S(1)}, bf16[144,576]{1,0:T(8,128)(2,1)S(1)}, u32[]{:S(2)}, u32[]{:S(2)}) collective-permute-start(bf16[144,576]{1,0:T(8,128)(2,1)S(1)} %fusion.110), channel_id=1, source_target_pairs={{0,16},{4,20},{8,24},{12,28},{16,0},{20,4},{24,8},{28,12},{1,17},{... | collective-permute-start | bytes 497672 | tf_op jit(solution)/shard_map/ppermute | solution.py:19
  207.7 20.6 %copy-start.26 = (f32[288,288]{1,0:T(8,128)S(1)}, f32[288,288]{1,0:T(8,128)}, u32[]{:S(2)}) copy-start(f32[288,288]{1,0:T(8,128)} %param.13) | copy-start | bytes 995332
  207.7 20.6 %copy-start.27 = (f32[288,288]{1,0:T(8,128)S(1)}, f32[288,288]{1,0:T(8,128)}, u32[]{:S(2)}) copy-start(f32[288,288]{1,0:T(8,128)} %param.15) | copy-start | bytes 995332
  207.7 20.6 %copy-start.28 = (f32[288,288]{1,0:T(8,128)S(1)}, f32[288,288]{1,0:T(8,128)}, u32[]{:S(2)}) copy-start(f32[288,288]{1,0:T(8,128)} %param.14) | copy-start | bytes 995332
  207.7 15.6 %collective-permute-start.28 = (bf16[144,576]{1,0:T(8,128)(2,1)S(1)}, bf16[144,576]{1,0:T(8,128)(2,1)S(1)}, u32[]{:S(2)}, u32[]{:S(2)}) collective-permute-start(bf16[144,576]{1,0:T(8,128)(2,1)S(1)} %fusion.111), channel_id=1, source_target_pairs={{0,16},{4,20},{8,24},{12,28},{16,0},{20,4},{24,8},{28,12},{1,17},{... | collective-permute-start | bytes 497672 | tf_op jit(solution)/shard_map/ppermute | solution.py:19
  220.9 5.7 %collective-permute-start.24 = (bf16[144,288]{1,0:T(8,128)(2,1)S(1)}, bf16[144,288]{1,0:T(8,128)(2,1)S(1)}, u32[]{:S(2)}, u32[]{:S(2)}) collective-permute-start(bf16[144,288]{1,0:T(8,128)(2,1)S(1)} %select_convert_fusion.7), channel_id=1, source_target_pairs={{0,8},{4,12},{8,0},{12,4},{16,24},{20,28},{24,16},{28,20},{1,9},{5... | collective-permute-start | bytes 248840 | tf_op jit(solution)/shard_map/ppermute | solution.py:19
  223.5 4.8 %collective-permute-start.29 = (bf16[144,288]{1,0:T(8,128)(2,1)S(1)}, bf16[144,288]{1,0:T(8,128)(2,1)S(1)}, u32[]{:S(2)}, u32[]{:S(2)}) collective-permute-start(bf16[144,288]{1,0:T(8,128)(2,1)S(1)} %select_convert_fusion.6), channel_id=1, source_target_pairs={{0,8},{4,12},{8,0},{12,4},{16,24},{20,28},{24,16},{28,20},{1,9},{5... | collective-permute-start | bytes 248840 | tf_op jit(solution)/shard_map/ppermute | solution.py:19
  (11 other events, 14.8 us)
